TPU v7x, 128 devices: a whole 4x4x4 slice. The times are simulated.
128 devices in a mesh: gx: 16 (over z_lo, y, core), gy: 8 (over z_hi, x).
Axes of the slice: x: 4, y: 4, z: 4 (z_hi: 2, z_lo: 2; z = z_hi * 2 + z_lo), core: 2. Of those that a mesh axis runs over, the one named last changes fastest.
Arguments:
- hopping_blocks: float32 [512, 5, 128, 128], P('gx'), may hold values from -0.5 to 0.5, as said below
- neighbors: int32 [512, 5], P('gx'), may hold values from 0 to 511, as said below
- orbital_grid: int32 [3, 65536], P(None, 'gx'), may hold values from 0 to 63
- trial_block: float32 [65536, 512], P('gx', 'gy'), may hold values from -6 to 6
Outputs:
- orthonormal_block: float32 [65536, 512], P('gx', 'gy')
- projected: float32 [512, 512], P('gx', 'gy')
- dipoles: float32 [3, 512, 512], P(None, 'gx', 'gy')
- spectrum: float32 [256], replicated
Inputs may be any that keep to these rules, and one draw needn't show every extreme that they name: `neighbors`: row block i names each of the column blocks i - 2, i - 1, i, i + 1, i + 2 once, in an order of its own, each clamped to 0 to 511. `hopping_blocks`: H is symmetric: block k of row block i is the transpose of the block of row block neighbors[i, k] that refers back to i, and the block of a row block with itself is symmetric; a block whose unclamped column block lies outside 0 to 511 is zero.
All inputs are finite; a program needn't handle non-finite values.
Results may differ from a plain program's by a relative error of at most 0.0003.
Values sent between devices are 32-bit elements; how exact they have to be, the bound alone decides.
No kernel may reach another device: no remote copies, remote signals or barrier semaphores. Data moves between devices by JAX's collectives and lax.ppermute only.
A program may use at most 320 MiB of HBM per device.

v0:
```python
import functools
import math

import jax
import jax.numpy as jnp
from jax import lax
from jax.experimental import pallas as pl
from jax.experimental.pallas import tpu as pltpu
f32=jnp.float32; bf16=jnp.bfloat16
MB=1<<20

def split(x):
    hi = x.astype(bf16)
    return hi, (x - hi.astype(f32)).astype(bf16)

def inv_chol_128(read, write):
    lane = lax.broadcasted_iota(jnp.int32,(8,128),1)
    sub = lax.broadcasted_iota(jnp.int32,(8,128),0)
    full = lambda v: jnp.broadcast_to(v,(8,128))
    m = [read(g) for g in range(16)]
    for p in range(16):
        j0 = 8*p
        d = m[p]
        c = [full(d[:,j0+l:j0+l+1]) for l in range(8)]
        s = {}; rp = []; rows = []; fin = d
        inpanel = (lane>=j0)&(lane<j0+8)
        for l in range(8):
            piv = full(c[l][l:l+1,:])
            r = 1.0/piv
            rp.append(r)
            mult = jnp.where(sub>l,c[l]*r,0.0)
            for q in range(l+1,8):
                s[l,q] = full(c[q][l:l+1,:])
                c[q] = c[q]-mult*s[l,q]
            row = jnp.where(lane==j0+l,1.0,full(d[l:l+1,:]))
            row = jnp.where(inpanel&(lane>j0+l),0.0,row)
            rows.append(row)
            d = jnp.where((lane==j0+l)&(sub>l),0.0,d)-mult*row
            fin = jnp.where(sub==l,row*lax.rsqrt(piv),fin)
        m[p] = fin
        for g in range(p+1,16):
            v = m[g]
            cg = [full(v[:,j0+l:j0+l+1]) for l in range(8)]
            v = jnp.where(inpanel,0.0,v)
            for l in range(8):
                mult = cg[l]*rp[l]
                for q in range(l+1,8):
                    cg[q] = cg[q]-mult*s[l,q]
                v = v-mult*rows[l]
            m[g] = v
    for g in range(16):
        write(g, jnp.where(lane<=sub+8*g, m[g], 0.0))

def hdot(a,b,dims):
    return lax.dot_general(a,b,(dims,((),())),precision=lax.Precision.HIGHEST,preferred_element_type=f32)

def chol_kernel(scale, g_ref, out_ref):
    for c in range(2):
        out_ref[:,256*c:256*c+256] = g_ref[:,c].reshape(512,256)*scale
    for k in range(4):
        k0 = 128*k
        def read(g): return out_ref[k0+8*g:k0+8*g+8,k0:k0+128]
        def write(g,v): out_ref[k0+8*g:k0+8*g+8,k0:k0+128] = v
        inv_chol_128(read,write)
        x = out_ref[128*k:128*k+128,128*k:128*k+128]
        for j in range(4):
            if j==k: continue
            out_ref[128*k:128*k+128,128*j:128*j+128] = hdot(x,out_ref[128*k:128*k+128,128*j:128*j+128],((1,),(0,)))
        bk = out_ref[128*k:128*k+128,:]
        for i in range(k+1,4):
            w = bk[:,128*i:128*i+128]
            upd = hdot(w,bk,((0,),(0,)))
            for j in range(4):
                if k<j<i: continue
                o = -upd[:,128*j:128*j+128] if j==k else out_ref[128*i:128*i+128,128*j:128*j+128]-upd[:,128*j:128*j+128]
                out_ref[128*i:128*i+128,128*j:128*j+128]=o
        for j in range(k+1,4):
            out_ref[128*k:128*k+128,128*j:128*j+128]=jnp.zeros((128,128),f32)

def call(kernel, name, args, outs, flops, scratch=(), vmem=16):
    single = not isinstance(outs,(list,tuple))
    if vmem < 56:
        whole = lambda v: pl.BlockSpec(memory_space=pltpu.VMEM)
        grid = {}
    else:
        whole = lambda v: pl.BlockSpec(v.shape, lambda g: (0,)*len(v.shape))
        grid = dict(grid=(1,))
    return pl.pallas_call(kernel, name=name, **grid,
        in_specs=[pl.BlockSpec(memory_space=pltpu.SMEM) if v.ndim==1 else whole(v) for v in args],
        out_specs=whole(outs) if single else [whole(v) for v in outs],
        out_shape=outs, scratch_shapes=list(scratch),
        cost_estimate=pl.CostEstimate(flops=flops,bytes_accessed=4*MB,transcendentals=0),
        compiler_params=pltpu.CompilerParams(vmem_limit_bytes=vmem*MB))(*args)

def sds(*shape, dtype=f32):
    return jax.ShapeDtypeStruct(shape,dtype)

def chol(g, scale):
    return call(functools.partial(chol_kernel,scale),"chol",(g,),sds(512,512),8000000000,vmem=56)

def dup_pack(y):
    lane = lax.broadcasted_iota(jnp.int32,y.shape,1)
    hi = y.astype(bf16).astype(f32)
    return jnp.where(lane<64, hi, y-hi).astype(bf16)

def prep_kernel(pos, h_ref, v_ref, a2_ref, y_ref, p_ref, own_ref):
    for r in range(4):
        for k in range(5):
            hi, lo = split(h_ref[r,k])
            a2_ref[r,0:128,128*k:128*k+128] = hi
            a2_ref[r,128:256,128*k:128*k+128] = lo
    @pl.when(pl.program_id(0)==pos[2])
    def _():
        own_ref[...] = a2_ref[...]
    v = v_ref[...]
    y = jnp.concatenate([v,v],axis=0).T
    y_ref[...] = y
    p_ref[...] = dup_pack(y)

def prep(pos, h, vt):
    B = pl.BlockSpec
    yb = B((512,128),lambda g,n:(g,0))
    sds = jax.ShapeDtypeStruct
    return pl.pallas_call(prep_kernel, name="prep",
        grid_spec=pltpu.PrefetchScalarGridSpec(num_scalar_prefetch=1, grid=(8,),
            in_specs=[B((4,5,128,128),lambda g,n:(g,0,0,0)), B((64,512),lambda g,n:(0,g))],
            out_specs=[B((4,256,640),lambda g,n:(g,0,0)), yb, yb, B((4,256,640),lambda g,n:(0,0,0))]),
        out_shape=[sds((32,256,640),bf16), sds((4096,128),f32), sds((4096,128),bf16), sds((4,256,640),bf16)],
        cost_estimate=pl.CostEstimate(flops=1000000,bytes_accessed=25*MB,transcendentals=0),
        compiler_params=pltpu.CompilerParams(vmem_limit_bytes=24*MB))(pos,h,vt)

def payload_kernel(pos, near, ha, hb, va, vb, grid, up_ref, down_ref, g_ref):
    g = grid[...].astype(f32)
    g_ref[...] = g
    base = 32*(2*pos[0]+pos[1])
    for out, h, v, n in ((up_ref,ha,va,30),(down_ref,hb,vb,0)):
        for r in range(2):
            for k in range(5):
                o = near[k,n+r]-base-(n+r)+2
                out[pl.ds(pl.multiple_of(640*r+128*o,128),128),:] = h[r,k]
        for b in range(4):
            out[1280+64*b:1344+64*b,:] = v[:,128*b:128*b+128]
        out[1536:1568,:] = jnp.zeros((32,128),f32)
        for u in range(4):
            out[1539+8*u:1542+8*u,:] = g[:,128*u:128*u+128]

def payload(pos, near, h, vt, grid):
    B = pl.BlockSpec
    w = lambda shape,*idx: B(shape, lambda g,p,n: idx)
    sds = jax.ShapeDtypeStruct
    return pl.pallas_call(payload_kernel, name="payload",
        grid_spec=pltpu.PrefetchScalarGridSpec(num_scalar_prefetch=2, grid=(1,),
            in_specs=[w((2,5,128,128),15,0,0,0),w((2,5,128,128),0,0,0,0),w((64,512),0,7),w((64,512),0,0),B((3,512),lambda g,p,n:(0,p[2]))],
            out_specs=[w((1568,128),0,0)]*2+[w((3,512),0,0)]),
        out_shape=[sds((1568,128),f32)]*2+[sds((3,512),f32)],
        cost_estimate=pl.CostEstimate(flops=1000000,bytes_accessed=4*MB,transcendentals=0),
        compiler_params=pltpu.CompilerParams(vmem_limit_bytes=56*MB))(pos,near,h,h,vt,vt,grid)

def halo_prep_kernel(lo_ref, hi_ref, a2_ref, y_ref, p_ref):
    for s, ref in ((0,lo_ref),(1,hi_ref)):
        for r in range(2):
            for k in range(5):
                at = 128*(5*r+k)
                hi, lo = split(ref[at:at+128,:])
                a2_ref[2*s+r,0:128,128*k:128*k+128] = hi
                a2_ref[2*s+r,128:256,128*k:128*k+128] = lo
        for b in range(4):
            v = ref[1280+64*b:1344+64*b,:]
            y = jnp.concatenate([v,v],axis=0).T
            p_ref[512*s+128*b:512*s+128*b+128,:] = dup_pack(y)
            e = b-2 if s==0 else b
            if 0<=e<2: y_ref[256*s+128*e:256*s+128*e+128,:] = y

def halo_prep(lo, hi):
    return pl.pallas_call(halo_prep_kernel, name="halo_prep",
        out_shape=[jax.ShapeDtypeStruct((4,256,640),bf16), jax.ShapeDtypeStruct((512,128),f32), jax.ShapeDtypeStruct((1024,128),bf16)],
        cost_estimate=pl.CostEstimate(flops=1000000,bytes_accessed=4*MB,transcendentals=0),
        compiler_params=pltpu.CompilerParams(vmem_limit_bytes=16*MB))(lo,hi)

def unpack_kernel(lo_ref, hi_ref, y_ref, p_ref):
    lane = lax.broadcasted_iota(jnp.int32,(128,128),1)
    for s, ref in ((0,lo_ref),(1,hi_ref)):
        for h in range(2):
            x = ref[128*h:128*h+128,:]; xr = pltpu.roll(x,64,1)
            pair = (jnp.where(lane<64,x,xr),jnp.where(lane<64,xr,x))
            for w in range(2):
                b = 2*h+w
                p_ref[512*s+128*b:512*s+128*b+128,:] = dup_pack(pair[w])
                e = b-2 if s==0 else b
                if 0<=e<2: y_ref[256*s+128*e:256*s+128*e+128,:] = pair[w]

def unpack(lo, hi):
    return pl.pallas_call(unpack_kernel, name="unpack",
        out_shape=[jax.ShapeDtypeStruct((512,128),f32), jax.ShapeDtypeStruct((1024,128),bf16)],
        cost_estimate=pl.CostEstimate(flops=1000000,bytes_accessed=MB,transcendentals=0),
        compiler_params=pltpu.CompilerParams(vmem_limit_bytes=16*MB))(lo,hi)

C0, HALF = -0.3, 0.9

def apply_row(a2, pieces):
    rhs = jnp.concatenate(pieces,axis=0)
    res = jnp.dot(a2, rhs, preferred_element_type=f32)
    u = res[:128]+res[128:]
    return u + pltpu.roll(u, 64, 1)

def recur(hy, y, yp):
    t = (hy - C0*y)/HALF
    return t if yp is None else 2.0*t - yp

def local(pos, near, i, k):
    return near[k,i]-32*(2*pos[0]+pos[1])

def slot_of(n):
    return jnp.where(n<0,n+36,jnp.where(n>31,n+4,n))

HALO_SLOTS = ((32,33,34,35,0),(33,34,35,0,1),(30,31,36,37,38),(31,36,37,38,39))

def block(ref, slot):
    return ref[pl.ds(pl.multiple_of(slot*128,128),128),:]

def step_kernel(first, wide, last, pos, near, a2, a2h, p, ph, y, yh, *rest):
    rest = list(rest); ext = rest.pop()
    yp = yph = None
    if not first:
        yp = rest.pop(0); yph = rest.pop(0)
    outs = rest
    g = pl.program_id(0)
    @pl.when(g==0)
    def _():
        ext[0:4096,:] = p[...]
        if wide: ext[4096:5120,:] = ph[...]
        else: ext[4352:4864,:] = ph[...]
    @pl.when(g<8)
    def _():
        for r in range(4):
            hy = apply_row(a2[r],[block(ext,slot_of(local(pos,near,4*g+r,k))) for k in range(5)])
            sl = slice(128*r,128*r+128)
            new = recur(hy,y[sl,:],None if first else yp[sl,:])
            if last:
                outs[0][0,:,sl] = new.T[:64]
            else:
                outs[0][sl,:] = new
                outs[1][sl,:] = dup_pack(new)
    if wide:
        @pl.when(g==8)
        def _():
            for r in range(4):
                hy = apply_row(a2h[r],[ext[128*b:128*b+128,:] for b in HALO_SLOTS[r]])
                sl = slice(128*r,128*r+128)
                new = recur(hy,yh[sl,:],None if first else yph[sl,:])
                outs[2][sl,:] = new
                outs[3][sl,:] = dup_pack(new)

def step(pos, near, a2, a2h, p, ph, y, yh, yp=None, yph=None, wide=False, last=False):
    first = yp is None
    B = pl.BlockSpec
    at = lambda g: jnp.minimum(g,7)
    w = lambda *shape: B(shape, lambda g,p,n: (0,)*len(shape))
    yb = B((512,128),lambda g,p,n:(at(g),0))
    sds = jax.ShapeDtypeStruct
    if last:
        outs=[B((1,64,512),lambda g,p,n:(at(g),0,0))]; shapes=[sds((8,64,512),f32)]
    else:
        outs=[yb,yb]; shapes=[sds((4096,128),f32),sds((4096,128),bf16)]
    if wide:
        outs+=[w(512,128)]*2; shapes+=[sds((512,128),f32),sds((512,128),bf16)]
    return pl.pallas_call(functools.partial(step_kernel,first,wide,last), name="step",
        grid_spec=pltpu.PrefetchScalarGridSpec(num_scalar_prefetch=2, grid=(9 if wide else 8,),
            in_specs=[B((4,256,640),lambda g,p,n:(at(g),0,0)), w(4,256,640), w(4096,128), w(*ph.shape), yb, w(512,128)]+([] if first else [yb,w(512,128)]),
            out_specs=outs, scratch_shapes=[pltpu.VMEM((5120,128),bf16)]),
        out_shape=shapes,
        cost_estimate=pl.CostEstimate(flops=36*2*256*640*128*4,bytes_accessed=16*MB,transcendentals=0),
        compiler_params=pltpu.CompilerParams(vmem_limit_bytes=24*MB))(
            pos,near,a2,a2h,p,ph,y,yh,*([] if first else [yp,yph]))

def edge_kernel(pos, near, alo, ahi, vlo, vhi, ph, ylo, yhi, plo, phi, ye, slo, shi, ext):
    lane = lax.broadcasted_iota(jnp.int32,(128,128),1)
    ext[0:256,:] = ph[0:256,:]
    ext[256:1024,:] = vlo[0:768,:]
    ext[1024:1792,:] = vhi[256:1024,:]
    ext[1792:2048,:] = ph[256:512,:]
    new = []
    for e in range(8):
        a, yr, pr = (alo,ylo,plo) if e<4 else (ahi,yhi,phi)
        hy = apply_row(a[e%4],[block(ext,local(pos,near,e if e<4 else 24+e,k)+(2 if e<4 else -18)) for k in range(5)])
        sl = slice(128*(e%4),128*(e%4)+128)
        new.append(recur(hy,yr[sl,:],pr[sl,:]))
        ye[128*e:128*e+128,:] = new[-1]
    for h in range(2):
        slo[128*h:128*h+128,:] = jnp.where(lane<64,new[2*h],new[2*h+1])
        shi[128*h:128*h+128,:] = jnp.where(lane<64,new[4+2*h],new[5+2*h])

def edge(pos, near, a2, p, ph, y, yp):
    B = pl.BlockSpec
    w = lambda shape,*idx: B(shape, lambda g,p,n: idx)
    ys = [w((512,128),0,0), w((512,128),7,0)]
    sds = jax.ShapeDtypeStruct
    return pl.pallas_call(edge_kernel, name="edge",
        grid_spec=pltpu.PrefetchScalarGridSpec(num_scalar_prefetch=2, grid=(1,),
            in_specs=[w((4,256,640),0,0,0), w((4,256,640),7,0,0), w((1024,128),0,0), w((1024,128),3,0), w((512,128),0,0)]+ys+ys,
            out_specs=[w((1024,128),0,0), w((256,128),0,0), w((256,128),0,0)],
            scratch_shapes=[pltpu.VMEM((2048,128),bf16)]),
        out_shape=[sds((1024,128),f32)]+[sds((256,128),f32)]*2,
        cost_estimate=pl.CostEstimate(flops=8*2*256*640*128,bytes_accessed=5*MB,transcendentals=0),
        compiler_params=pltpu.CompilerParams(vmem_limit_bytes=24*MB))(
            pos,near,a2,a2,p,p,ph,y,y,yp,yp)

def inner_kernel(pos, near, a2, p, ye, y, yp, yo, po):
    g = pl.program_id(0)
    @pl.when((g==0)|(g==7))
    def _():
        new = ye[...]
        yo[...] = new
        po[...] = dup_pack(new)
    @pl.when((g>0)&(g<7))
    def _():
        for r in range(4):
            hy = apply_row(a2[r],[block(p,local(pos,near,4*g+r,k)) for k in range(5)])
            sl = slice(128*r,128*r+128)
            new = recur(hy,y[sl,:],yp[sl,:])
            yo[sl,:] = new
            po[sl,:] = dup_pack(new)

def inner(pos, near, a2, p, ye, y, yp):
    B = pl.BlockSpec
    yb = B((512,128),lambda g,p,n:(g,0))
    sds = jax.ShapeDtypeStruct
    return pl.pallas_call(inner_kernel, name="inner",
        grid_spec=pltpu.PrefetchScalarGridSpec(num_scalar_prefetch=2, grid=(8,),
            in_specs=[B((4,256,640),lambda g,p,n:(g,0,0)), B((4096,128),lambda g,p,n:(0,0)), B((512,128),lambda g,p,n:(g//7,0)), yb, yb],
            out_specs=[yb,yb]),
        out_shape=[sds((4096,128),f32),sds((4096,128),bf16)],
        cost_estimate=pl.CostEstimate(flops=24*2*256*640*128*4,bytes_accessed=16*MB,transcendentals=0),
        compiler_params=pltpu.CompilerParams(vmem_limit_bytes=24*MB))(pos,near,a2,p,ye,y,yp)

NT = ((1,),(1,))
NN = ((1,),(0,))
NORB = 65536

def bdot(a, b, dims):
    return lax.dot_general(a,b,(dims,((),())),preferred_element_type=f32)

def params(mb):
    return pltpu.CompilerParams(vmem_limit_bytes=mb*MB)

SMEM = pl.BlockSpec(memory_space=pltpu.SMEM)
VMEM = pl.BlockSpec(memory_space=pltpu.VMEM)

def gram_kernel(pos, x_ref, o_ref, g_ref):
    half = pl.ds(pl.multiple_of(256*pos[1],256),256)
    xs = [split(x_ref[...]),split(o_ref[...])]
    hs = [split(x_ref[half,:]),split(o_ref[half,:])]
    for i in range(2):
        sl = slice(256*i,256*i+256)
        s = None
        for (xh,xl),(hh,hl) in zip(xs,hs):
            t = bdot(xh[sl],hh,NT)+bdot(xl[sl],hh,NT)+bdot(xh[sl],hl,NT)
            s = t if s is None else s+t
        g_ref[32*i:32*i+32] = s.reshape(32,8,256)

def gram(pos, x, o):
    return call(gram_kernel,"gram",(pos,x,o),sds(64,8,256),3*2*512**3)

def applied_kernel(pos, near, x_ref, hi_ref, a2, yt, xh, xl):
    for ref, at, w in ((x_ref,0,512),(hi_ref,512,256)):
        h, l = split(ref[...])
        xh[:,at:at+w] = h; xl[:,at:at+w] = l
    xh[:,512:768] = xh[:,512:768]*2; xl[:,512:768] = xl[:,512:768]*2
    xh[:,768:896] = jnp.zeros((512,128),bf16); xl[:,768:896] = jnp.zeros((512,128),bf16)
    for i in range(4):
        n = [local(pos,near,4*pos[2]+i,k)-4*pos[2] for k in range(5)]
        at = [pl.ds(pl.multiple_of(jnp.where(m<0,6,m)*128,128),128) for m in n]
        h = jnp.concatenate([xh[:,a] for a in at],axis=1)
        l = jnp.concatenate([xl[:,a] for a in at],axis=1)
        r = bdot(h,a2[i],NT)
        yt[:,128*i:128*i+128] = r[:,:128]+r[:,128:]+bdot(l,a2[i,:128,:],NT)

def applied(pos, near, x, hi, a2):
    B = pl.BlockSpec
    w = lambda shape: B(shape, lambda g,p,n: (0,)*len(shape))
    return pl.pallas_call(applied_kernel, name="applied",
        grid_spec=pltpu.PrefetchScalarGridSpec(num_scalar_prefetch=2, grid=(1,),
            in_specs=[w((512,512)),w((512,256)),w((4,256,640))],
            out_specs=w((512,512)),
            scratch_shapes=[pltpu.VMEM((512,896),bf16),pltpu.VMEM((512,896),bf16)]),
        out_shape=jax.ShapeDtypeStruct((512,512),f32),
        cost_estimate=pl.CostEstimate(flops=4*2*512*512*640,bytes_accessed=5*MB,transcendentals=0),
        compiler_params=params(24))(pos,near,x,hi,a2)

def moment_kernel(pos, x_ref, o_ref, yt_ref, ot_ref, g_ref, lo_ref, hi_ref, s_ref, acc):
    c = pos[1]
    xs = [split(x_ref[...]),split(o_ref[...])]
    tail = jnp.where(c==0,hi_ref[...],lo_ref[...])
    og = jnp.concatenate([tail[8*u+3:8*u+6,:] for u in range(4)],axis=1)
    for q in range(2):
        ws = []
        for x, y, g in ((x_ref,yt_ref,g_ref[...]),(o_ref,ot_ref,og)):
            places = (g+0.5)/32.0-1.0
            if q==0:
                w = jnp.where(c==0,y[...],x[...]*places[1:2,:])
            else:
                w = x[...]*jnp.where(c==0,places[0:1,:],places[2:3,:])
            ws.append(split(w))
        for i in range(2):
            sl = slice(256*i,256*i+256)
            s = None
            for (xh,xl),(yh,yl) in zip(xs,ws):
                t = bdot(xh[sl],yh,NT)+bdot(xl[sl],yh,NT)+bdot(xh[sl],yl,NT)
                s = t if s is None else s+t
            if q==0: acc[sl,:] = s
            else: s_ref[32*i:32*i+32,8:16,:] = s.reshape(32,8,512)
        if q==0:
            for i in range(4):
                sl = slice(128*i,128*i+128)
                s_ref[16*i:16*i+16,0:8,:] = (0.5*(acc[sl,:]+acc[:,sl].T)).reshape(16,8,512)

def moments(pos, x, o, yt, ot, g, lo, hi):
    B = pl.BlockSpec
    w = lambda shape,*idx: B(shape, lambda g: idx)
    full = w((512,512),0,0)
    return pl.pallas_call(moment_kernel, name="moments", grid=(1,),
        in_specs=[SMEM]+[full]*4+[w((3,512),0,0),w((32,128),48,0),w((32,128),48,0)],
        out_specs=w((64,16,512),0,0,0), scratch_shapes=[pltpu.VMEM((512,512),f32)],
        out_shape=jax.ShapeDtypeStruct((64,16,512),f32),
        cost_estimate=pl.CostEstimate(flops=12*2*512**3,bytes_accessed=8*MB,transcendentals=0),
        compiler_params=params(40))(pos,x,o,yt,ot,g,lo,hi)

def total_kernel(p_ref, o_ref):
    o_ref[...] = jnp.broadcast_to(jnp.sum(p_ref[...],axis=0)[None],o_ref.shape)

def total(part):
    return call(total_kernel,"total",(part,),sds(128,8,256),200000)

def half_kernel(pos, s_ref, li_ref, out_ref, lt):
    lane = lax.broadcasted_iota(jnp.int32,(8,128),1)
    sub = lax.broadcasted_iota(jnp.int32,(8,128),0)
    z = hdot(jnp.sum(s_ref[...],axis=0),li_ref[...],NT)
    z0 = z[0:8]; z1 = z[8:16]
    k = 8*pos[0]+pos[2]
    lt[...] = li_ref[:,pl.ds(pl.multiple_of((k//16)*128,128),128)].T
    e = jnp.sum(z0*lt[pl.ds(pl.multiple_of(8*(k%16),8),8),:],axis=0,keepdims=True)
    ee = jnp.zeros((8,128),f32)
    for g in range(8):
        b = jnp.broadcast_to(e[:,128*(g//2):128*(g//2)+128],(8,128))
        if g%2==0: b = pltpu.roll(b,64,1)
        ee = jnp.where(sub==g,b,ee)
    for u in range(4):
        for v in range(4):
            a = z0[:,128*u:128*u+128]; b = z1[:,128*u:128*u+128]
            if v: a = pltpu.roll(a,128-32*v,1)
            if v!=1: b = pltpu.roll(b,(160-32*v)%128,1)
            t = jnp.where(lane<32,a,jnp.where(lane<64,b,ee))
            for y in range(8):
                out_ref[8*(4*u+v)+y] = t

def half(pos, s, li):
    return call(half_kernel,"half",(pos,s,li),sds(128,8,128),2*24*512*512*6,[pltpu.VMEM((128,512),f32)],vmem=24)

def tile_kernel(pos, r_ref, li_ref, p_ref, d_ref, w_ref, e_ref, acc):
    c = pos[1]; gx = 2*pos[0]+c; gy = pos[2]
    lane = lax.broadcasted_iota(jnp.int32,(64,128),1)
    lane8 = lax.broadcasted_iota(jnp.int32,(8,128),1)
    lb = li_ref[pl.ds(pl.multiple_of(64*gy,64),64),:]
    t0 = hdot(lb,r_ref[:,0].reshape(512,128),NN)
    t1 = hdot(lb,r_ref[:,1].reshape(512,128),NN)
    t = jnp.where(lane<64,t0,pltpu.roll(t1,64,1))
    tt = jnp.concatenate([t,t],axis=0).T
    p_ref[...] = tt[0:32,0:64]*(1.0/NORB)
    for q in range(3):
        d_ref[q] = tt[32*q+32:32*q+64,0:64]*(1.0/math.sqrt(NORB))
    e = jnp.sum(r_ref[:,0].reshape(64,8,128),axis=0)
    e_ref[...] = e*(1.0/NORB)
    ea = jnp.broadcast_to(e_ref[pl.ds(pos[0],1),:],(8,128))
    ea = pltpu.roll(ea,64-32*c,1)
    ea = jnp.where(lane8<32,ea,0.0)
    ea = ea+pltpu.roll(ea,32,1)+pltpu.roll(ea,64,1)+pltpu.roll(ea,96,1)
    eb = pltpu.roll(jnp.broadcast_to(e_ref[pl.ds(gy,1),:],(8,128)),64,1)
    eb = jnp.broadcast_to(eb[0:1,:],(128,128)).T[0:64,:]
    gap = eb-jnp.broadcast_to(ea[0:1,:],(64,128))
    dip = t*(1.0/math.sqrt(NORB))
    sq = jnp.where(lane>=32,dip*dip,0.0)
    st = (sq+pltpu.roll(sq,32,1)+pltpu.roll(sq,64,1)+pltpu.roll(sq,96,1))*(0.01/math.pi)
    base = (64*(lane8//32)).astype(f32)+0.5
    for w in range(64):
        om = -0.3+0.6*(base+float(w))/256.0
        tot = jnp.zeros((8,128),f32)
        for b in range(8):
            x = om-gap[8*b:8*b+8,:]
            tot = tot+st[8*b:8*b+8,:]/(x*x+0.0001)
        acc[w:w+1,:] = jnp.sum(tot,axis=0,keepdims=True)
    sel = (lane8//32==lax.broadcasted_iota(jnp.int32,(8,128),0)).astype(f32)
    m = hdot(sel,jnp.concatenate([acc[...],acc[...]],axis=0),NT)*(1.0/(512.0*512.0))
    m = jnp.concatenate([jnp.where(lane8[0:1]<64,m[0:1],m[1:2]),jnp.where(lane8[0:1]<64,m[2:3],m[3:4])],axis=0)
    w_ref[...] = jnp.broadcast_to(m[None],(128,2,128))

def tile(pos, r, li):
    return call(tile_kernel,"tile",(pos,r,li),[sds(32,64),sds(3,32,64),sds(128,2,128)],10000000,[pltpu.VMEM((8,128),f32),pltpu.VMEM((64,128),f32)],vmem=24)

def rotate_kernel(pos, x_ref, li_ref, *o_refs):
    xh, xl = split(x_ref[...])
    for i in range(4):
        at = [pl.ds(pl.multiple_of(64*jnp.bitwise_xor(pos[2],2*i+j),64),64) for j in range(2)]
        lh, ll = split(jnp.concatenate([li_ref[a,:] for a in at],axis=0))
        o = bdot(lh,xh,NN)+bdot(ll,xh,NN)+bdot(lh,xl,NN)
        o_refs[2*i][...] = o[0:64]; o_refs[2*i+1][...] = o[64:128]

def rotate(pos, x, li):
    return call(rotate_kernel,"rotate",(pos,x,li),[sds(64,512)]*8,3*2*512**3,vmem=56)

def gather_kernel(pos, *refs):
    for r in range(8):
        refs[8][:,pl.ds(pl.multiple_of(512*jnp.bitwise_xor(pos[2],r),512),512)] = refs[r][...]

def gather(pos, pieces):
    return call(gather_kernel,"gather",(pos,*pieces),sds(64,4096),1000)

SLABS = ("gq","c")
PEERS = ("gq","gy")
ALL = ("gq","c","gy")

def swap(x, axis):
    return lax.all_to_all(x,axis,split_axis=0,concat_axis=0,tiled=True)

def chain(n):
    return [(i,i+1) for i in range(n-1)], [(i+1,i) for i in range(n-1)]

def shards(hopping_blocks, neighbors, orbital_grid, trial_block):
    gq = lax.axis_index("gq"); c = lax.axis_index("c"); gy = lax.axis_index("gy")
    pos = jnp.stack([gq,c,gy])
    near = neighbors.T
    up, down = chain(16)
    vt = trial_block.T
    sup, sdown, grid = payload(pos,near,hopping_blocks,vt,orbital_grid)
    plo = lax.ppermute(sup,SLABS,up)
    phi = lax.ppermute(sdown,SLABS,down)
    a2, y0, p0, own = prep(pos,hopping_blocks,vt)
    a2h, y0h, p0h = halo_prep(plo,phi)
    y1, p1, y1h, p1h = step(pos,near,a2,a2h,p0,p0h,y0,y0h,wide=True)
    ye, slo, shi = edge(pos,near,a2,p1,p1h,y1,y0)
    lo = lax.ppermute(shi,SLABS,up)
    hi = lax.ppermute(slo,SLABS,down)
    y2, p2 = inner(pos,near,a2,p1,ye,y1,y0)
    y2h, p2h = unpack(lo,hi)
    y3, p3, y3h, p3h = step(pos,near,a2,a2h,p2,p2h,y2,y2h,y1,y1h,wide=True)
    sent, = step(pos,near,a2,a2h,p3,p3h,y3,y3h,y2,y2h,last=True)

    x = swap(sent,"gy").reshape(512,512)
    pair = [(i,i^1) for i in range(16)]
    other = lax.ppermute(x,SLABS,pair)
    hi = lax.ppermute(x[:,:256],ALL,chain(128)[1])
    part = gram(pos,x,other)
    part, xa = lax.optimization_barrier((part,x))
    yt = applied(pos,near,xa,hi,own)
    summed, yt = lax.optimization_barrier((swap(part,PEERS),yt))
    ot = lax.ppermute(yt,SLABS,[(i+1,i) for i in range(0,16,2)])
    both, ot = lax.optimization_barrier((total(summed),ot))
    g = swap(both,ALL).reshape(8,2,64,256)
    s = moments(pos,x,other,yt,ot,grid,plo,phi)
    s, g = lax.optimization_barrier((s,g))
    li = chol(g,1.0/NORB)
    rows = swap(half(pos,swap(s,PEERS),li),ALL).reshape(8,2,64,128)
    projected, dipoles, spec = tile(pos,rows,li)
    q = rotate(pos,x,li)
    q = [q[0]]+[lax.ppermute(q[r],"gy",[(i,i^r) for i in range(8)]) for r in range(1,8)]
    orthonormal = gather(pos,q).T
    spectrum = jnp.sum(swap(spec,ALL),axis=0).reshape(256)
    return orthonormal, projected, dipoles, spectrum

def solution(mesh):
    P = jax.sharding.PartitionSpec
    fine = jax.sharding.Mesh(mesh.devices.reshape(8,2,8),ALL)
    return jax.shard_map(shards, mesh=fine,
        in_specs=(P(SLABS,None,None,None),P(SLABS,None),P(None,SLABS),P(SLABS,"gy")),
        out_specs=(P(SLABS,"gy"),P(SLABS,"gy"),P(None,SLABS,"gy"),P()),
        check_vma=False)
```

profile of v0, /device:TPU:1, one launch (start us, length us, event | category | flops | bytes accessed | tf_op | source)
XLA Modules:
  0.0 234.6 jit_solution(1051578732617549240)
XLA Ops:
  1.3 3.5 %payload.1 = (f32[1568,128]{1,0:T(8,128)}, f32[1568,128]{1,0:T(8,128)}, f32[3,512]{1,0:T(4,128)}) custom-call(s32[3]{0:T(128)} %pad_add_fusion.pos, s32[5,32]{1,0:T(8,128)} %bitcast.20, f32[32,5,128,128]{3,2,1,0:T(8,128)} %hb.1, f32[32,5,128,128]{3,2,1,0:T(8,128)} %hb.1, f32[64,4096]{1,0:T(8,128)} %bitcast.10, f32[64,4096]{1,0:T(8,128)} %bitcast.11, ...), custom_call_target="tpu_custom_call" | custom-call | flops 1000000 | bytes 4194304 | tf_op jit(solution)/shard_map/payload/pallas_call | solution.py:151
  4.7 4.6 %collective-permute-start = (f32[1568,128]{1,0:T(8,128)}, f32[1568,128]{1,0:T(8,128)S(1)}, u32[]{:S(2)}, u32[]{:S(2)}) collective-permute-start(f32[1568,128]{1,0:T(8,128)} %get-tuple-element.49), channel_id=1, source_target_pairs={{0,8},{8,16},{16,24},{24,32},{32,40},{40,48},{48,56},{56,64},{64,7... | collective-permute-start | bytes 2408456 | tf_op jit(solution)/shard_map/ppermute | solution.py:534
  11.3 4.0 %copy-done = f32[32,5,128,128]{3,2,1,0:T(8,128)S(1)} copy-done((f32[32,5,128,128]{3,2,1,0:T(8,128)S(1)}, f32[32,5,128,128]{3,2,1,0:T(8,128)}, u32[]{:S(2)}) %copy-start) | copy-done | bytes 10485784
  15.3 3.6 %prep.1 = (bf16[32,256,640]{2,1,0:T(8,128)(2,1)S(1)}, f32[4096,128]{1,0:T(8,128)S(1)}, bf16[4096,128]{1,0:T(8,128)(2,1)S(1)}, bf16[4,256,640]{2,1,0:T(8,128)(2,1)S(1)}) custom-call(s32[3]{0:T(128)S(1)} %copy-done.9, f32[32,5,128,128]{3,2,1,0:T(8,128)S(1)} %copy-done, f32[64,4096]{1,0:T(8,128)S(1)} %bitcast.12), custom_call_target="tpu_custom_call" | custom-call | flops 1000000 | bytes 26214400 | tf_op jit(solution)/shard_map/prep/pallas_call | solution.py:124
  18.9 4.1 %collective-permute-done.1.hi_ref = f32[1568,128]{1,0:T(8,128)S(1)} collective-permute-done((f32[1568,128]{1,0:T(8,128)}, f32[1568,128]{1,0:T(8,128)S(1)}, u32[]{:S(2)}, u32[]{:S(2)}) %collective-permute-start.1) | collective-permute-done | bytes 802848 | tf_op jit(solution)/shard_map/ppermute | solution.py:535
  23.4 6.2 %step.3 = (f32[4096,128]{1,0:T(8,128)S(1)}, bf16[4096,128]{1,0:T(8,128)(2,1)S(1)}, f32[512,128]{1,0:T(8,128)S(1)}, bf16[512,128]{1,0:T(8,128)(2,1)S(1)}) custom-call(s32[3]{0:T(128)S(1)} %copy-done.9, s32[5,32]{1,0:T(8,128)S(1)} %bitcast.21, bf16[32,256,640]{2,1,0:T(8,128)(2,1)S(1)} %get-tuple-element.48.a2.alo.ahi, ...), custom_call_target="tpu_custom_call" | custom-call | flops 6039797760 | bytes 16777216 | tf_op jit(solution)/shard_map/step/pallas_call | solution.py:267
  35.5 4.4 %inner.1 = (f32[4096,128]{1,0:T(8,128)S(1)}, bf16[4096,128]{1,0:T(8,128)(2,1)S(1)}) custom-call(s32[3]{0:T(128)S(1)} %copy-done.9, s32[5,32]{1,0:T(8,128)S(1)} %bitcast.23, bf16[32,256,640]{2,1,0:T(8,128)(2,1)S(1)} %get-tuple-element.48.a2.alo.ahi, bf16[4096,128]{1,0:T(8,128)(2,1)S(1)} %get-tuple-element.56.vlo.vhi.p, f32[1024,128]{1,0:T(8,128)S(1)} %get-tuple-element.59.ye, ...), custom_call_target="tpu_custom_call" | custom-call | flops 4026531840 | bytes 16777216 | tf_op jit(solution)/shard_map/inner/pallas_call | solution.py:328
  40.1 6.2 %step.4 = (f32[4096,128]{1,0:T(8,128)S(1)}, bf16[4096,128]{1,0:T(8,128)(2,1)S(1)}, f32[512,128]{1,0:T(8,128)S(1)}, bf16[512,128]{1,0:T(8,128)(2,1)S(1)}) custom-call(s32[3]{0:T(128)S(1)} %copy-done.9, s32[5,32]{1,0:T(8,128)S(1)} %bitcast.24, bf16[32,256,640]{2,1,0:T(8,128)(2,1)S(1)} %get-tuple-element.48.a2.alo.ahi, ...), custom_call_target="tpu_custom_call" | custom-call | flops 6039797760 | bytes 16777216 | tf_op jit(solution)/shard_map/step/pallas_call | solution.py:267
  46.4 5.9 %step.5 = f32[8,64,512]{2,1,0:T(8,128)S(1)} custom-call(s32[3]{0:T(128)S(1)} %copy-done.9, s32[5,32]{1,0:T(8,128)S(1)} %bitcast.25, bf16[32,256,640]{2,1,0:T(8,128)(2,1)S(1)} %get-tuple-element.48.a2.alo.ahi, bf16[4,256,640]{2,1,0:T(8,128)(2,1)S(1)} %get-tuple-element.51.a2h, bf16[4096,128]{1,0:T(8,128)(2,1)S(1)} %get-tuple-element.67.p, ...), custom_call_target="tpu_custom_call" | custom-call | flops 6039797760 | bytes 16777216 | tf_op jit(solution)/shard_map/step/pallas_call | solution.py:267
  52.3 24.8 %all_to_all.30 = f32[8,64,512]{2,1,0:T(8,128)S(1)} all-to-all(f32[8,64,512]{2,1,0:T(8,128)S(1)} %step.5), channel_id=1, replica_groups=mesh['gq'=8,'c'=2,'gy'=8] {'gy'}, dimensions={0} | all-to-all | bytes 2097152 | tf_op jit(solution)/shard_map/all_to_all | solution.py:522
  85.0 8.9 %all-to-all-start.1 = ((f32[64,8,256]{2,1,0:T(8,128)}), f32[64,8,256]{2,1,0:T(8,128)S(1)}, u32[]{:S(2)}, u32[]{:S(2)}) async-start(f32[64,8,256]{2,1,0:T(8,128)} %copy-done.6), calls=%async_computation.1 | async-start | bytes 1048576 | tf_op jit(solution)/shard_map/all_to_all | solution.py:522
  95.5 3.8 %applied.1.yt_ref = f32[512,512]{1,0:T(8,128)S(1)} custom-call(s32[3]{0:T(128)S(1)} %copy-done.9, s32[5,32]{1,0:T(8,128)S(1)} %bitcast.26, f32[512,512]{1,0:T(8,128)S(1)} %bitcast.16, f32[512,256]{1,0:T(8,128)} %collective-permute-done.5.hi_ref, bf16[4,256,640]{2,1,0:T(8,128)(2,1)S(1)} %copy-done.12), custom_call_target="tpu_custom_call" | custom-call | flops 1342177280 | bytes 5242880 | tf_op jit(solution)/shard_map/applied/pallas_call | solution.py:381
  100.2 4.9 %all-to-all-done.1.p_ref = f32[64,8,256]{2,1,0:T(8,128)S(1)} async-done(((f32[64,8,256]{2,1,0:T(8,128)}), f32[64,8,256]{2,1,0:T(8,128)S(1)}, u32[]{:S(2)}, u32[]{:S(2)}) %all-to-all-start.1) | async-done | bytes 524320 | tf_op jit(solution)/shard_map/all_to_all | solution.py:522
  105.1 4.7 %collective-permute-start.6 = (f32[512,512]{1,0:T(8,128)}, f32[512,512]{1,0:T(8,128)S(1)}, u32[]{:S(2)}, u32[]{:S(2)}) collective-permute-start(f32[512,512]{1,0:T(8,128)} %copy-done.15), channel_id=1, source_target_pairs={{8,0},{24,16},{40,32},{56,48},{72,64},{88,80},{104,96},{120,112},{... | collective-permute-start | bytes 3145736 | tf_op jit(solution)/shard_map/ppermute | solution.py:555
  113.2 18.5 %all-to-all-start.2 = ((f32[128,8,256]{2,1,0:T(8,128)}), f32[128,8,256]{2,1,0:T(8,128)}, u32[]{:S(2)}, u32[]{:S(2)}) async-start(f32[128,8,256]{2,1,0:T(8,128)} %total.1), calls=%async_computation.2 | async-start | bytes 2097152 | tf_op jit(solution)/shard_map/all_to_all | solution.py:522
  135.4 4.1 %moments.1 = f32[64,16,512]{2,1,0:T(8,128)S(1)} custom-call(s32[3]{0:T(128)S(1)} %copy-done.9, f32[512,512]{1,0:T(8,128)S(1)} %bitcast.17, f32[512,512]{1,0:T(8,128)S(1)} %copy-done.14, f32[512,512]{1,0:T(8,128)S(1)} %copy-done.16, f32[512,512]{1,0:T(8,128)S(1)} %copy-done.18, f32[3,512]{1,0:T(4,128)S(1)} %copy-done.19, ...), custom_call_target="tpu_custom_call" | custom-call | flops 3221225472 | bytes 8388608 | tf_op jit(solution)/shard_map/moments/pallas_call | solution.py:421
  140.9 8.3 %all-to-all-done.2 = f32[128,8,256]{2,1,0:T(8,128)} async-done(((f32[128,8,256]{2,1,0:T(8,128)}), f32[128,8,256]{2,1,0:T(8,128)}, u32[]{:S(2)}, u32[]{:S(2)}) %all-to-all-start.2) | async-done | bytes 1048608 | tf_op jit(solution)/shard_map/all_to_all | solution.py:522
  149.2 5.9 %all-to-all-start.3 = ((f32[64,16,512]{2,1,0:T(8,128)}), f32[64,16,512]{2,1,0:T(8,128)S(1)}, u32[]{:S(2)}, u32[]{:S(2)}) async-start(f32[64,16,512]{2,1,0:T(8,128)} %copy-done.5), calls=%async_computation.3 | async-start | bytes 4194304 | tf_op jit(solution)/shard_map/all_to_all | solution.py:522
  155.1 21.3 %chol.1.li_ref = f32[512,512]{1,0:T(8,128)} custom-call(f32[8,2,64,256]{3,2,1,0:T(8,128)} %bitcast.6.g_ref), custom_call_target="tpu_custom_call" | custom-call | flops 8000000000 | bytes 4194304 | tf_op jit(solution)/shard_map/chol/pallas_call | solution.py:88
  176.4 6.0 %all-to-all-done.3.s_ref = f32[64,16,512]{2,1,0:T(8,128)S(1)} async-done(((f32[64,16,512]{2,1,0:T(8,128)}), f32[64,16,512]{2,1,0:T(8,128)S(1)}, u32[]{:S(2)}, u32[]{:S(2)}) %all-to-all-start.3) | async-done | bytes 2097184 | tf_op jit(solution)/shard_map/all_to_all | solution.py:522
  186.2 7.3 %all-to-all-start.4 = ((f32[128,8,128]{2,1,0:T(8,128)}), f32[128,8,128]{2,1,0:T(8,128)S(1)}, u32[]{:S(2)}, u32[]{:S(2)}) async-start(f32[128,8,128]{2,1,0:T(8,128)} %half.1), calls=%async_computation.4 | async-start | bytes 1048576 | tf_op jit(solution)/shard_map/all_to_all | solution.py:522
  203.9 6.0 %collective-permute-start.12 = (f32[64,512]{1,0:T(8,128)}, f32[64,512]{1,0:T(8,128)S(1)}, u32[]{:S(2)}, u32[]{:S(2)}) collective-permute-start(f32[64,512]{1,0:T(8,128)} %get-tuple-element.86), channel_id=1, source_target_pairs={{0,6},{1,7},{2,4},{3,5},{4,2},{5,3},{6,0},{7,1},{8,14},{9,15},{10,... | collective-permute-start | bytes 393224 | tf_op jit(solution)/shard_map/ppermute | solution.py:564
  214.1 9.5 %all-to-all-start.5 = ((f32[128,2,128]{2,1,0:T(2,128)}), f32[128,2,128]{2,1,0:T(2,128)S(1)}, u32[]{:S(2)}, u32[]{:S(2)}) async-start(f32[128,2,128]{2,1,0:T(2,128)} %get-tuple-element.91), calls=%async_computation.5 | async-start | bytes 262144 | tf_op jit(solution)/shard_map/all_to_all | solution.py:522
  226.2 7.3 %all-to-all-done.5 = f32[128,2,128]{2,1,0:T(2,128)S(1)} async-done(((f32[128,2,128]{2,1,0:T(2,128)}), f32[128,2,128]{2,1,0:T(2,128)S(1)}, u32[]{:S(2)}, u32[]{:S(2)}) %all-to-all-start.5) | async-done | bytes 131104 | tf_op jit(solution)/shard_map/all_to_all | solution.py:522
  (76 shorter events, 49.3 us)
Async XLA Ops:
  4.7 14.2 %collective-permute-start = (f32[1568,128]{1,0:T(8,128)}, f32[1568,128]{1,0:T(8,128)S(1)}, u32[]{:S(2)}, u32[]{:S(2)}) collective-permute-start(f32[1568,128]{1,0:T(8,128)} %get-tuple-element.49), channel_id=1, source_target_pairs={{0,8},{8,16},{16,24},{24,32},{32,40},{40,48},{48,56},{56,64},{64,7... | collective-permute-start | bytes 2408456 | tf_op jit(solution)/shard_map/ppermute | solution.py:534
  9.3 13.7 %collective-permute-start.1 = (f32[1568,128]{1,0:T(8,128)}, f32[1568,128]{1,0:T(8,128)S(1)}, u32[]{:S(2)}, u32[]{:S(2)}) collective-permute-start(f32[1568,128]{1,0:T(8,128)} %get-tuple-element.50), channel_id=1, source_target_pairs={{8,0},{16,8},{24,16},{32,24},{40,32},{48,40},{56,48},{64,56},{72,6... | collective-permute-start | bytes 2408456 | tf_op jit(solution)/shard_map/ppermute | solution.py:535
  18.9 10.7 %copy-start.11 = (bf16[4,256,640]{2,1,0:T(8,128)(2,1)}, bf16[4,256,640]{2,1,0:T(8,128)(2,1)S(1)}, u32[]{:S(2)}) copy-start(bf16[4,256,640]{2,1,0:T(8,128)(2,1)S(1)} %get-tuple-element.73.a2) | copy-start | bytes 3932164
  31.1 8.8 %collective-permute-start.2 = (f32[256,128]{1,0:T(8,128)S(1)}, f32[256,128]{1,0:T(8,128)S(1)}, u32[]{:S(2)}, u32[]{:S(2)}) collective-permute-start(f32[256,128]{1,0:T(8,128)S(1)} %get-tuple-element.61), channel_id=1, source_target_pairs={{0,8},{8,16},{16,24},{24,32},{32,40},{40,48},{48,56},{56,64},{64,7... | collective-permute-start | bytes 393224 | tf_op jit(solution)/shard_map/ppermute | solution.py:540
  33.1 6.9 %collective-permute-start.3 = (f32[256,128]{1,0:T(8,128)S(1)}, f32[256,128]{1,0:T(8,128)S(1)}, u32[]{:S(2)}, u32[]{:S(2)}) collective-permute-start(f32[256,128]{1,0:T(8,128)S(1)} %get-tuple-element.62), channel_id=1, source_target_pairs={{8,0},{16,8},{24,16},{32,24},{40,32},{48,40},{56,48},{64,56},{72,6... | collective-permute-start | bytes 393224 | tf_op jit(solution)/shard_map/ppermute | solution.py:541
  77.1 54.7 %copy-start.4 = (f32[8,64,512]{2,1,0:T(8,128)}, f32[8,64,512]{2,1,0:T(8,128)S(1)}, u32[]{:S(2)}) copy-start(f32[8,64,512]{2,1,0:T(8,128)S(1)} %all_to_all.30) | copy-start | bytes 3145732
  77.1 4.5 %collective-permute-start.4 = (f32[512,512]{1,0:T(8,128)S(1)}, f32[512,512]{1,0:T(8,128)S(1)}, u32[]{:S(2)}, u32[]{:S(2)}) collective-permute-start(f32[512,512]{1,0:T(8,128)S(1)} %bitcast.13), channel_id=1, source_target_pairs={{0,8},{8,0},{16,24},{24,16},{32,40},{40,32},{48,56},{56,48},{64,72... | collective-permute-start | bytes 3145736 | tf_op jit(solution)/shard_map/ppermute | solution.py:549
  78.4 15.7 %collective-permute-start.5 = (f32[512,256]{1,0:T(8,128)}, f32[512,256]{1,0:T(8,128)}, u32[]{:S(2)}, u32[]{:S(2)}) collective-permute-start(f32[512,256]{1,0:T(8,128)} %slice.4), channel_id=1, source_target_pairs={{1,0},{2,1},{3,2},{4,3},{5,4},{6,5},{7,6},{8,7},{9,8},{10,9},{11,1... | collective-permute-start | bytes 1572872 | tf_op jit(solution)/shard_map/ppermute | solution.py:550
  85.0 20.2 %all-to-all-start.1 = ((f32[64,8,256]{2,1,0:T(8,128)}), f32[64,8,256]{2,1,0:T(8,128)S(1)}, u32[]{:S(2)}, u32[]{:S(2)}) async-start(f32[64,8,256]{2,1,0:T(8,128)} %copy-done.6), calls=%async_computation.1 | async-start | bytes 1048576 | tf_op jit(solution)/shard_map/all_to_all | solution.py:522
  100.2 31.5 %copy-start.19 = (f32[3,512]{1,0:T(4,128)S(1)}, f32[3,512]{1,0:T(4,128)}, u32[]{:S(2)}) copy-start(f32[3,512]{1,0:T(4,128)} %get-tuple-element.77.g_ref) | copy-start | bytes 18436
  105.1 7.1 %collective-permute-start.6 = (f32[512,512]{1,0:T(8,128)}, f32[512,512]{1,0:T(8,128)S(1)}, u32[]{:S(2)}, u32[]{:S(2)}) collective-permute-start(f32[512,512]{1,0:T(8,128)} %copy-done.15), channel_id=1, source_target_pairs={{8,0},{24,16},{40,32},{56,48},{72,64},{88,80},{104,96},{120,112},{... | collective-permute-start | bytes 3145736 | tf_op jit(solution)/shard_map/ppermute | solution.py:555
  113.2 36.0 %all-to-all-start.2 = ((f32[128,8,256]{2,1,0:T(8,128)}), f32[128,8,256]{2,1,0:T(8,128)}, u32[]{:S(2)}, u32[]{:S(2)}) async-start(f32[128,8,256]{2,1,0:T(8,128)} %total.1), calls=%async_computation.2 | async-start | bytes 2097152 | tf_op jit(solution)/shard_map/all_to_all | solution.py:522
  149.2 33.3 %all-to-all-start.3 = ((f32[64,16,512]{2,1,0:T(8,128)}), f32[64,16,512]{2,1,0:T(8,128)S(1)}, u32[]{:S(2)}, u32[]{:S(2)}) async-start(f32[64,16,512]{2,1,0:T(8,128)} %copy-done.5), calls=%async_computation.3 | async-start | bytes 4194304 | tf_op jit(solution)/shard_map/all_to_all | solution.py:522
  186.2 25.3 %copy-start.3 = (f32[512,512]{1,0:T(8,128)S(1)}, f32[512,512]{1,0:T(8,128)}, u32[]{:S(2)}) copy-start(f32[512,512]{1,0:T(8,128)} %chol.1.li_ref) | copy-start | bytes 3145732
  186.2 25.3 %copy-start.10 = (s32[3]{0:T(128)S(1)}, s32[3]{0:T(128)}, u32[]{:S(2)}) copy-start(s32[3]{0:T(128)} %pad_add_fusion.pos) | copy-start | bytes 40
  186.2 25.3 %all-to-all-start.4 = ((f32[128,8,128]{2,1,0:T(8,128)}), f32[128,8,128]{2,1,0:T(8,128)S(1)}, u32[]{:S(2)}, u32[]{:S(2)}) async-start(f32[128,8,128]{2,1,0:T(8,128)} %half.1), calls=%async_computation.4 | async-start | bytes 1048576 | tf_op jit(solution)/shard_map/all_to_all | solution.py:522
  196.8 7.1 %collective-permute-start.7 = (f32[64,512]{1,0:T(8,128)}, f32[64,512]{1,0:T(8,128)S(1)}, u32[]{:S(2)}, u32[]{:S(2)}) collective-permute-start(f32[64,512]{1,0:T(8,128)} %get-tuple-element.81), channel_id=1, source_target_pairs={{0,1},{1,0},{2,3},{3,2},{4,5},{5,4},{6,7},{7,6},{8,9},{9,8},{10,11... | collective-permute-start | bytes 393224 | tf_op jit(solution)/shard_map/ppermute | solution.py:564
  198.2 11.8 %collective-permute-start.8 = (f32[64,512]{1,0:T(8,128)}, f32[64,512]{1,0:T(8,128)S(1)}, u32[]{:S(2)}, u32[]{:S(2)}) collective-permute-start(f32[64,512]{1,0:T(8,128)} %get-tuple-element.82), channel_id=1, source_target_pairs={{0,2},{1,3},{2,0},{3,1},{4,6},{5,7},{6,4},{7,5},{8,10},{9,11},{10,... | collective-permute-start | bytes 393224 | tf_op jit(solution)/shard_map/ppermute | solution.py:564
  200.6 23.1 %collective-permute-start.9 = (f32[64,512]{1,0:T(8,128)}, f32[64,512]{1,0:T(8,128)S(1)}, u32[]{:S(2)}, u32[]{:S(2)}) collective-permute-start(f32[64,512]{1,0:T(8,128)} %get-tuple-element.83), channel_id=1, source_target_pairs={{0,3},{1,2},{2,1},{3,0},{4,7},{5,6},{6,5},{7,4},{8,11},{9,10},{10,... | collective-permute-start | bytes 393224 | tf_op jit(solution)/shard_map/ppermute | solution.py:564
  200.6 23.0 %collective-permute-start.10 = (f32[64,512]{1,0:T(8,128)}, f32[64,512]{1,0:T(8,128)S(1)}, u32[]{:S(2)}, u32[]{:S(2)}) collective-permute-start(f32[64,512]{1,0:T(8,128)} %get-tuple-element.84), channel_id=1, source_target_pairs={{0,4},{1,5},{2,6},{3,7},{4,0},{5,1},{6,2},{7,3},{8,12},{9,13},{10,... | collective-permute-start | bytes 393224 | tf_op jit(solution)/shard_map/ppermute | solution.py:564
  203.9 19.7 %collective-permute-start.11 = (f32[64,512]{1,0:T(8,128)}, f32[64,512]{1,0:T(8,128)S(1)}, u32[]{:S(2)}, u32[]{:S(2)}) collective-permute-start(f32[64,512]{1,0:T(8,128)} %get-tuple-element.85), channel_id=1, source_target_pairs={{0,5},{1,4},{2,7},{3,6},{4,1},{5,0},{6,3},{7,2},{8,13},{9,12},{10,... | collective-permute-start | bytes 393224 | tf_op jit(solution)/shard_map/ppermute | solution.py:564
  203.9 19.7 %collective-permute-start.12 = (f32[64,512]{1,0:T(8,128)}, f32[64,512]{1,0:T(8,128)S(1)}, u32[]{:S(2)}, u32[]{:S(2)}) collective-permute-start(f32[64,512]{1,0:T(8,128)} %get-tuple-element.86), channel_id=1, source_target_pairs={{0,6},{1,7},{2,4},{3,5},{4,2},{5,3},{6,0},{7,1},{8,14},{9,15},{10,... | collective-permute-start | bytes 393224 | tf_op jit(solution)/shard_map/ppermute | solution.py:564
  210.0 13.7 %collective-permute-start.13 = (f32[64,512]{1,0:T(8,128)}, f32[64,512]{1,0:T(8,128)S(1)}, u32[]{:S(2)}, u32[]{:S(2)}) collective-permute-start(f32[64,512]{1,0:T(8,128)} %get-tuple-element.87), channel_id=1, source_target_pairs={{0,7},{1,6},{2,5},{3,4},{4,3},{5,2},{6,1},{7,0},{8,15},{9,14},{10,... | collective-permute-start | bytes 393224 | tf_op jit(solution)/shard_map/ppermute | solution.py:564
  214.1 19.4 %all-to-all-start.5 = ((f32[128,2,128]{2,1,0:T(2,128)}), f32[128,2,128]{2,1,0:T(2,128)S(1)}, u32[]{:S(2)}, u32[]{:S(2)}) async-start(f32[128,2,128]{2,1,0:T(2,128)} %get-tuple-element.91), calls=%async_computation.5 | async-start | bytes 262144 | tf_op jit(solution)/shard_map/all_to_all | solution.py:522
  (15 other events, 44.4 us)
where the time goes:
time: 238 us; the launch traced here: 235 us
  starting transfers between devices  84.1 us (35%)
  Pallas kernels  73.8 us (31%)
  waiting for transfers between devices  32.1 us (13%)
  blocking collectives  24.8 us (10%)
  local copies, waits for them, and re-layouts  17.1 us (7%)
    all_to_all x5, starting transfers between devices, swap(): return lax.all_to_all(x, axis, split_axis=0, concat_axis=0, tiled=True)  50.2 us
    pallas_call x7, Pallas kernels, call(): pl.pallas_call(kernel, name=name, **grid, in_specs=[pl.BlockSpec(memory_s...  33.9 us
    all_to_all x5, waiting for transfers between devices, swap(): return lax.all_to_all(x, axis, split_axis=0, concat_axis=0, tiled=True)  26.5 us
    all_to_all x1, blocking collectives, swap(): return lax.all_to_all(x, axis, split_axis=0, concat_axis=0, tiled=True)  24.8 us
    pallas_call x3, Pallas kernels, step(): pl.pallas_call(functools.partial(step_kernel, first, wide, last), name='s...  18.3 us
    unnamed x40, local copies, waits for them, and re-layouts  16.2 us
    ppermute x7, starting transfers between devices, shards(): lax.ppermute(q[r], 'gy', [(i, i ^ r) for i in range(8)])  14.7 us
  transfers between devices with their start and end apart: 19, of which 7 were waited for; matrix products, arithmetic and copies ran while one was open for 0% of the time, Pallas kernels for 20%

commit v1 on v0

--- a/solution.py
+++ b/solution.py
@@ -57,25 +57,25 @@
 def chol_kernel(scale, g_ref, out_ref):
     for c in range(2):
         out_ref[:,256*c:256*c+256] = g_ref[:,c].reshape(512,256)*scale
-    for k in range(4):
-        k0 = 128*k
-        def read(g): return out_ref[k0+8*g:k0+8*g+8,k0:k0+128]
-        def write(g,v): out_ref[k0+8*g:k0+8*g+8,k0:k0+128] = v
+    column = lax.broadcasted_iota(jnp.int32,(128,512),1)//128
+    def outer(k, carry):
+        k0 = pl.multiple_of(k*128,128)
+        rows = pl.ds(k0,128)
+        def read(g): return out_ref[pl.ds(k0+8*g,8),rows]
+        def write(g,v): out_ref[pl.ds(k0+8*g,8),rows] = v
         inv_chol_128(read,write)
-        x = out_ref[128*k:128*k+128,128*k:128*k+128]
-        for j in range(4):
-            if j==k: continue
-            out_ref[128*k:128*k+128,128*j:128*j+128] = hdot(x,out_ref[128*k:128*k+128,128*j:128*j+128],((1,),(0,)))
-        bk = out_ref[128*k:128*k+128,:]
-        for i in range(k+1,4):
-            w = bk[:,128*i:128*i+128]
-            upd = hdot(w,bk,((0,),(0,)))
-            for j in range(4):
-                if k<j<i: continue
-                o = -upd[:,128*j:128*j+128] if j==k else out_ref[128*i:128*i+128,128*j:128*j+128]-upd[:,128*j:128*j+128]
-                out_ref[128*i:128*i+128,128*j:128*j+128]=o
-        for j in range(k+1,4):
-            out_ref[128*k:128*k+128,128*j:128*j+128]=jnp.zeros((128,128),f32)
+        x = out_ref[rows,rows]
+        bk = jnp.where(column==k,jnp.concatenate([x]*4,axis=1),hdot(x,out_ref[rows,:],((1,),(0,))))
+        out_ref[rows,:] = bk
+        for i in range(1,4):
+            @pl.when(k<i)
+            def _():
+                at = slice(128*i,128*i+128)
+                upd = hdot(bk[:,at],bk,((0,),(0,)))
+                out_ref[at,:] = jnp.where(column==k,0.0,out_ref[at,:])-upd
+        out_ref[rows,:] = jnp.where(column<=k,bk,0.0)
+        return carry
+    lax.fori_loop(0,4,outer,0)
 
 def call(kernel, name, args, outs, flops, scratch=(), vmem=16):
     single = not isinstance(outs,(list,tuple))

time: 238 us -> 224 us (0.941); the launches traced: 235 us -> 223 us
  starting transfers between devices: 84.1 us -> 73 us
    all_to_all x5, starting transfers between devices: 50.2 us -> 39.1 us  [swap(): return lax.all_to_all(x, axis, split_axis=0, concat_axis=0, tiled=True)]
  transfers between devices with their start and end apart: 19 -> 19, of which waited for: 7 -> 7; matrix products, arithmetic and copies ran while one was open for 0% -> 0% of each run, Pallas kernels for 20% -> 22%
where the time goes in v1:
time: 224 us; the launch traced here: 223 us
  Pallas kernels  75.3 us (34%)
  starting transfers between devices  73 us (33%)
  waiting for transfers between devices  30.9 us (14%)
  blocking collectives  24.8 us (11%)
  local copies, waits for them, and re-layouts  17.1 us (8%)
    all_to_all x5, starting transfers between devices, swap(): return lax.all_to_all(x, axis, split_axis=0, concat_axis=0, tiled=True)  39.1 us
    pallas_call x7, Pallas kernels, call(): pl.pallas_call(kernel, name=name, **grid, in_specs=[pl.BlockSpec(memory_s...  35.4 us
    all_to_all x5, waiting for transfers between devices, swap(): return lax.all_to_all(x, axis, split_axis=0, concat_axis=0, tiled=True)  25.2 us
    all_to_all x1, blocking collectives, swap(): return lax.all_to_all(x, axis, split_axis=0, concat_axis=0, tiled=True)  24.8 us
    pallas_call x3, Pallas kernels, step(): pl.pallas_call(functools.partial(step_kernel, first, wide, last), name='s...  18.3 us
    unnamed x40, local copies, waits for them, and re-layouts  16.2 us
    ppermute x7, starting transfers between devices, shards(): lax.ppermute(q[r], 'gy', [(i, i ^ r) for i in range(8)])  14.7 us
    ppermute x1, starting transfers between devices, shards(): ot = lax.ppermute(yt, SLABS, [(i + 1, i) for i in range(0, 16, 2)])  4.65 us
  transfers between devices with their start and end apart: 19, of which 7 were waited for; matrix products, arithmetic and copies ran while one was open for 0% of the time, Pallas kernels for 22%

profile of v1, /device:TPU:1, one launch (start us, length us, event | category | flops | bytes accessed | tf_op | source)
XLA Modules:
  0.0 223.3 jit_solution(16377765472402977850)
XLA Ops:
  1.3 3.5 %payload.1 = (f32[1568,128]{1,0:T(8,128)}, f32[1568,128]{1,0:T(8,128)}, f32[3,512]{1,0:T(4,128)}) custom-call(s32[3]{0:T(128)} %pad_add_fusion.pos, s32[5,32]{1,0:T(8,128)} %bitcast.20, f32[32,5,128,128]{3,2,1,0:T(8,128)} %hb.1, f32[32,5,128,128]{3,2,1,0:T(8,128)} %hb.1, f32[64,4096]{1,0:T(8,128)} %bitcast.10, f32[64,4096]{1,0:T(8,128)} %bitcast.11, ...), custom_call_target="tpu_custom_call" | custom-call | flops 1000000 | bytes 4194304 | tf_op jit(solution)/shard_map/payload/pallas_call | solution.py:151
  4.7 4.6 %collective-permute-start = (f32[1568,128]{1,0:T(8,128)}, f32[1568,128]{1,0:T(8,128)S(1)}, u32[]{:S(2)}, u32[]{:S(2)}) collective-permute-start(f32[1568,128]{1,0:T(8,128)} %get-tuple-element.49), channel_id=1, source_target_pairs={{0,8},{8,16},{16,24},{24,32},{32,40},{40,48},{48,56},{56,64},{64,7... | collective-permute-start | bytes 2408456 | tf_op jit(solution)/shard_map/ppermute | solution.py:534
  11.3 4.0 %copy-done = f32[32,5,128,128]{3,2,1,0:T(8,128)S(1)} copy-done((f32[32,5,128,128]{3,2,1,0:T(8,128)S(1)}, f32[32,5,128,128]{3,2,1,0:T(8,128)}, u32[]{:S(2)}) %copy-start) | copy-done | bytes 10485784
  15.2 3.6 %prep.1 = (bf16[32,256,640]{2,1,0:T(8,128)(2,1)S(1)}, f32[4096,128]{1,0:T(8,128)S(1)}, bf16[4096,128]{1,0:T(8,128)(2,1)S(1)}, bf16[4,256,640]{2,1,0:T(8,128)(2,1)S(1)}) custom-call(s32[3]{0:T(128)S(1)} %copy-done.9, f32[32,5,128,128]{3,2,1,0:T(8,128)S(1)} %copy-done, f32[64,4096]{1,0:T(8,128)S(1)} %bitcast.12), custom_call_target="tpu_custom_call" | custom-call | flops 1000000 | bytes 26214400 | tf_op jit(solution)/shard_map/prep/pallas_call | solution.py:124
  18.9 4.1 %collective-permute-done.1.hi_ref = f32[1568,128]{1,0:T(8,128)S(1)} collective-permute-done((f32[1568,128]{1,0:T(8,128)}, f32[1568,128]{1,0:T(8,128)S(1)}, u32[]{:S(2)}, u32[]{:S(2)}) %collective-permute-start.1) | collective-permute-done | bytes 802848 | tf_op jit(solution)/shard_map/ppermute | solution.py:535
  23.4 6.2 %step.3 = (f32[4096,128]{1,0:T(8,128)S(1)}, bf16[4096,128]{1,0:T(8,128)(2,1)S(1)}, f32[512,128]{1,0:T(8,128)S(1)}, bf16[512,128]{1,0:T(8,128)(2,1)S(1)}) custom-call(s32[3]{0:T(128)S(1)} %copy-done.9, s32[5,32]{1,0:T(8,128)S(1)} %bitcast.21, bf16[32,256,640]{2,1,0:T(8,128)(2,1)S(1)} %get-tuple-element.48.a2.alo.ahi, ...), custom_call_target="tpu_custom_call" | custom-call | flops 6039797760 | bytes 16777216 | tf_op jit(solution)/shard_map/step/pallas_call | solution.py:267
  35.5 4.4 %inner.1 = (f32[4096,128]{1,0:T(8,128)S(1)}, bf16[4096,128]{1,0:T(8,128)(2,1)S(1)}) custom-call(s32[3]{0:T(128)S(1)} %copy-done.9, s32[5,32]{1,0:T(8,128)S(1)} %bitcast.23, bf16[32,256,640]{2,1,0:T(8,128)(2,1)S(1)} %get-tuple-element.48.a2.alo.ahi, bf16[4096,128]{1,0:T(8,128)(2,1)S(1)} %get-tuple-element.56.vlo.vhi.p, f32[1024,128]{1,0:T(8,128)S(1)} %get-tuple-element.59.ye, ...), custom_call_target="tpu_custom_call" | custom-call | flops 4026531840 | bytes 16777216 | tf_op jit(solution)/shard_map/inner/pallas_call | solution.py:328
  40.1 6.2 %step.4 = (f32[4096,128]{1,0:T(8,128)S(1)}, bf16[4096,128]{1,0:T(8,128)(2,1)S(1)}, f32[512,128]{1,0:T(8,128)S(1)}, bf16[512,128]{1,0:T(8,128)(2,1)S(1)}) custom-call(s32[3]{0:T(128)S(1)} %copy-done.9, s32[5,32]{1,0:T(8,128)S(1)} %bitcast.24, bf16[32,256,640]{2,1,0:T(8,128)(2,1)S(1)} %get-tuple-element.48.a2.alo.ahi, ...), custom_call_target="tpu_custom_call" | custom-call | flops 6039797760 | bytes 16777216 | tf_op jit(solution)/shard_map/step/pallas_call | solution.py:267
  46.4 5.9 %step.5 = f32[8,64,512]{2,1,0:T(8,128)S(1)} custom-call(s32[3]{0:T(128)S(1)} %copy-done.9, s32[5,32]{1,0:T(8,128)S(1)} %bitcast.25, bf16[32,256,640]{2,1,0:T(8,128)(2,1)S(1)} %get-tuple-element.48.a2.alo.ahi, bf16[4,256,640]{2,1,0:T(8,128)(2,1)S(1)} %get-tuple-element.51.a2h, bf16[4096,128]{1,0:T(8,128)(2,1)S(1)} %get-tuple-element.67.p, ...), custom_call_target="tpu_custom_call" | custom-call | flops 6039797760 | bytes 16777216 | tf_op jit(solution)/shard_map/step/pallas_call | solution.py:267
  52.3 24.8 %all_to_all.30 = f32[8,64,512]{2,1,0:T(8,128)S(1)} all-to-all(f32[8,64,512]{2,1,0:T(8,128)S(1)} %step.5), channel_id=1, replica_groups=mesh['gq'=8,'c'=2,'gy'=8] {'gy'}, dimensions={0} | all-to-all | bytes 2097152 | tf_op jit(solution)/shard_map/all_to_all | solution.py:522
  85.0 8.9 %all-to-all-start.1 = ((f32[64,8,256]{2,1,0:T(8,128)}), f32[64,8,256]{2,1,0:T(8,128)S(1)}, u32[]{:S(2)}, u32[]{:S(2)}) async-start(f32[64,8,256]{2,1,0:T(8,128)} %copy-done.6), calls=%async_computation.1 | async-start | bytes 1048576 | tf_op jit(solution)/shard_map/all_to_all | solution.py:522
  95.5 3.8 %applied.1.yt_ref = f32[512,512]{1,0:T(8,128)S(1)} custom-call(s32[3]{0:T(128)S(1)} %copy-done.9, s32[5,32]{1,0:T(8,128)S(1)} %bitcast.26, f32[512,512]{1,0:T(8,128)S(1)} %bitcast.16, f32[512,256]{1,0:T(8,128)} %collective-permute-done.5.hi_ref, bf16[4,256,640]{2,1,0:T(8,128)(2,1)S(1)} %copy-done.12), custom_call_target="tpu_custom_call" | custom-call | flops 1342177280 | bytes 5242880 | tf_op jit(solution)/shard_map/applied/pallas_call | solution.py:381
  100.2 4.9 %all-to-all-done.1.p_ref = f32[64,8,256]{2,1,0:T(8,128)S(1)} async-done(((f32[64,8,256]{2,1,0:T(8,128)}), f32[64,8,256]{2,1,0:T(8,128)S(1)}, u32[]{:S(2)}, u32[]{:S(2)}) %all-to-all-start.1) | async-done | bytes 524320 | tf_op jit(solution)/shard_map/all_to_all | solution.py:522
  105.1 4.7 %collective-permute-start.6 = (f32[512,512]{1,0:T(8,128)}, f32[512,512]{1,0:T(8,128)S(1)}, u32[]{:S(2)}, u32[]{:S(2)}) collective-permute-start(f32[512,512]{1,0:T(8,128)} %copy-done.15), channel_id=1, source_target_pairs={{8,0},{24,16},{40,32},{56,48},{72,64},{88,80},{104,96},{120,112},{... | collective-permute-start | bytes 3145736 | tf_op jit(solution)/shard_map/ppermute | solution.py:555
  113.2 7.5 %all-to-all-start.2 = ((f32[128,8,256]{2,1,0:T(8,128)}), f32[128,8,256]{2,1,0:T(8,128)}, u32[]{:S(2)}, u32[]{:S(2)}) async-start(f32[128,8,256]{2,1,0:T(8,128)} %total.1), calls=%async_computation.2 | async-start | bytes 2097152 | tf_op jit(solution)/shard_map/all_to_all | solution.py:522
  124.4 4.1 %moments.1 = f32[64,16,512]{2,1,0:T(8,128)S(1)} custom-call(s32[3]{0:T(128)S(1)} %copy-done.9, f32[512,512]{1,0:T(8,128)S(1)} %bitcast.17, f32[512,512]{1,0:T(8,128)S(1)} %copy-done.14, f32[512,512]{1,0:T(8,128)S(1)} %copy-done.16, f32[512,512]{1,0:T(8,128)S(1)} %copy-done.18, f32[3,512]{1,0:T(4,128)S(1)} %copy-done.19, ...), custom_call_target="tpu_custom_call" | custom-call | flops 3221225472 | bytes 8388608 | tf_op jit(solution)/shard_map/moments/pallas_call | solution.py:421
  129.8 8.5 %all-to-all-done.2 = f32[128,8,256]{2,1,0:T(8,128)} async-done(((f32[128,8,256]{2,1,0:T(8,128)}), f32[128,8,256]{2,1,0:T(8,128)}, u32[]{:S(2)}, u32[]{:S(2)}) %all-to-all-start.2) | async-done | bytes 1048608 | tf_op jit(solution)/shard_map/all_to_all | solution.py:522
  138.3 5.9 %all-to-all-start.3 = ((f32[64,16,512]{2,1,0:T(8,128)}), f32[64,16,512]{2,1,0:T(8,128)S(1)}, u32[]{:S(2)}, u32[]{:S(2)}) async-start(f32[64,16,512]{2,1,0:T(8,128)} %copy-done.5), calls=%async_computation.3 | async-start | bytes 4194304 | tf_op jit(solution)/shard_map/all_to_all | solution.py:522
  144.2 22.8 %chol.1.li_ref = f32[512,512]{1,0:T(8,128)} custom-call(f32[8,2,64,256]{3,2,1,0:T(8,128)} %bitcast.6.g_ref), custom_call_target="tpu_custom_call" | custom-call | flops 8000000000 | bytes 4194304 | tf_op jit(solution)/shard_map/chol/pallas_call | solution.py:88
  167.0 4.5 %all-to-all-done.3.s_ref = f32[64,16,512]{2,1,0:T(8,128)S(1)} async-done(((f32[64,16,512]{2,1,0:T(8,128)}), f32[64,16,512]{2,1,0:T(8,128)S(1)}, u32[]{:S(2)}, u32[]{:S(2)}) %all-to-all-start.3) | async-done | bytes 2097184 | tf_op jit(solution)/shard_map/all_to_all | solution.py:522
  175.3 7.3 %all-to-all-start.4 = ((f32[128,8,128]{2,1,0:T(8,128)}), f32[128,8,128]{2,1,0:T(8,128)S(1)}, u32[]{:S(2)}, u32[]{:S(2)}) async-start(f32[128,8,128]{2,1,0:T(8,128)} %half.1), calls=%async_computation.4 | async-start | bytes 1048576 | tf_op jit(solution)/shard_map/all_to_all | solution.py:522
  193.0 6.0 %collective-permute-start.12 = (f32[64,512]{1,0:T(8,128)}, f32[64,512]{1,0:T(8,128)S(1)}, u32[]{:S(2)}, u32[]{:S(2)}) collective-permute-start(f32[64,512]{1,0:T(8,128)} %get-tuple-element.86), channel_id=1, source_target_pairs={{0,6},{1,7},{2,4},{3,5},{4,2},{5,3},{6,0},{7,1},{8,14},{9,15},{10,... | collective-permute-start | bytes 393224 | tf_op jit(solution)/shard_map/ppermute | solution.py:564
  203.2 9.5 %all-to-all-start.5 = ((f32[128,2,128]{2,1,0:T(2,128)}), f32[128,2,128]{2,1,0:T(2,128)S(1)}, u32[]{:S(2)}, u32[]{:S(2)}) async-start(f32[128,2,128]{2,1,0:T(2,128)} %get-tuple-element.91), calls=%async_computation.5 | async-start | bytes 262144 | tf_op jit(solution)/shard_map/all_to_all | solution.py:522
  215.3 7.3 %all-to-all-done.5 = f32[128,2,128]{2,1,0:T(2,128)S(1)} async-done(((f32[128,2,128]{2,1,0:T(2,128)}), f32[128,2,128]{2,1,0:T(2,128)S(1)}, u32[]{:S(2)}, u32[]{:S(2)}) %all-to-all-start.5) | async-done | bytes 131104 | tf_op jit(solution)/shard_map/all_to_all | solution.py:522
  (76 shorter events, 49.3 us)
Async XLA Ops:
  4.7 14.2 %collective-permute-start = (f32[1568,128]{1,0:T(8,128)}, f32[1568,128]{1,0:T(8,128)S(1)}, u32[]{:S(2)}, u32[]{:S(2)}) collective-permute-start(f32[1568,128]{1,0:T(8,128)} %get-tuple-element.49), channel_id=1, source_target_pairs={{0,8},{8,16},{16,24},{24,32},{32,40},{40,48},{48,56},{56,64},{64,7... | collective-permute-start | bytes 2408456 | tf_op jit(solution)/shard_map/ppermute | solution.py:534
  9.3 13.7 %collective-permute-start.1 = (f32[1568,128]{1,0:T(8,128)}, f32[1568,128]{1,0:T(8,128)S(1)}, u32[]{:S(2)}, u32[]{:S(2)}) collective-permute-start(f32[1568,128]{1,0:T(8,128)} %get-tuple-element.50), channel_id=1, source_target_pairs={{8,0},{16,8},{24,16},{32,24},{40,32},{48,40},{56,48},{64,56},{72,6... | collective-permute-start | bytes 2408456 | tf_op jit(solution)/shard_map/ppermute | solution.py:535
  18.9 10.7 %copy-start.11 = (bf16[4,256,640]{2,1,0:T(8,128)(2,1)}, bf16[4,256,640]{2,1,0:T(8,128)(2,1)S(1)}, u32[]{:S(2)}) copy-start(bf16[4,256,640]{2,1,0:T(8,128)(2,1)S(1)} %get-tuple-element.73.a2) | copy-start | bytes 3932164
  31.1 8.8 %collective-permute-start.2 = (f32[256,128]{1,0:T(8,128)S(1)}, f32[256,128]{1,0:T(8,128)S(1)}, u32[]{:S(2)}, u32[]{:S(2)}) collective-permute-start(f32[256,128]{1,0:T(8,128)S(1)} %get-tuple-element.61), channel_id=1, source_target_pairs={{0,8},{8,16},{16,24},{24,32},{32,40},{40,48},{48,56},{56,64},{64,7... | collective-permute-start | bytes 393224 | tf_op jit(solution)/shard_map/ppermute | solution.py:540
  33.1 6.9 %collective-permute-start.3 = (f32[256,128]{1,0:T(8,128)S(1)}, f32[256,128]{1,0:T(8,128)S(1)}, u32[]{:S(2)}, u32[]{:S(2)}) collective-permute-start(f32[256,128]{1,0:T(8,128)S(1)} %get-tuple-element.62), channel_id=1, source_target_pairs={{8,0},{16,8},{24,16},{32,24},{40,32},{48,40},{56,48},{64,56},{72,6... | collective-permute-start | bytes 393224 | tf_op jit(solution)/shard_map/ppermute | solution.py:541
  77.1 43.6 %copy-start.4 = (f32[8,64,512]{2,1,0:T(8,128)}, f32[8,64,512]{2,1,0:T(8,128)S(1)}, u32[]{:S(2)}) copy-start(f32[8,64,512]{2,1,0:T(8,128)S(1)} %all_to_all.30) | copy-start | bytes 3145732
  77.1 4.5 %collective-permute-start.4 = (f32[512,512]{1,0:T(8,128)S(1)}, f32[512,512]{1,0:T(8,128)S(1)}, u32[]{:S(2)}, u32[]{:S(2)}) collective-permute-start(f32[512,512]{1,0:T(8,128)S(1)} %bitcast.13), channel_id=1, source_target_pairs={{0,8},{8,0},{16,24},{24,16},{32,40},{40,32},{48,56},{56,48},{64,72... | collective-permute-start | bytes 3145736 | tf_op jit(solution)/shard_map/ppermute | solution.py:549
  78.4 15.7 %collective-permute-start.5 = (f32[512,256]{1,0:T(8,128)}, f32[512,256]{1,0:T(8,128)}, u32[]{:S(2)}, u32[]{:S(2)}) collective-permute-start(f32[512,256]{1,0:T(8,128)} %slice.4), channel_id=1, source_target_pairs={{1,0},{2,1},{3,2},{4,3},{5,4},{6,5},{7,6},{8,7},{9,8},{10,9},{11,1... | collective-permute-start | bytes 1572872 | tf_op jit(solution)/shard_map/ppermute | solution.py:550
  85.0 20.2 %all-to-all-start.1 = ((f32[64,8,256]{2,1,0:T(8,128)}), f32[64,8,256]{2,1,0:T(8,128)S(1)}, u32[]{:S(2)}, u32[]{:S(2)}) async-start(f32[64,8,256]{2,1,0:T(8,128)} %copy-done.6), calls=%async_computation.1 | async-start | bytes 1048576 | tf_op jit(solution)/shard_map/all_to_all | solution.py:522
  100.2 20.4 %copy-start.19 = (f32[3,512]{1,0:T(4,128)S(1)}, f32[3,512]{1,0:T(4,128)}, u32[]{:S(2)}) copy-start(f32[3,512]{1,0:T(4,128)} %get-tuple-element.77.g_ref) | copy-start | bytes 18436
  105.1 7.1 %collective-permute-start.6 = (f32[512,512]{1,0:T(8,128)}, f32[512,512]{1,0:T(8,128)S(1)}, u32[]{:S(2)}, u32[]{:S(2)}) collective-permute-start(f32[512,512]{1,0:T(8,128)} %copy-done.15), channel_id=1, source_target_pairs={{8,0},{24,16},{40,32},{56,48},{72,64},{88,80},{104,96},{120,112},{... | collective-permute-start | bytes 3145736 | tf_op jit(solution)/shard_map/ppermute | solution.py:555
  113.2 25.1 %all-to-all-start.2 = ((f32[128,8,256]{2,1,0:T(8,128)}), f32[128,8,256]{2,1,0:T(8,128)}, u32[]{:S(2)}, u32[]{:S(2)}) async-start(f32[128,8,256]{2,1,0:T(8,128)} %total.1), calls=%async_computation.2 | async-start | bytes 2097152 | tf_op jit(solution)/shard_map/all_to_all | solution.py:522
  138.3 33.3 %all-to-all-start.3 = ((f32[64,16,512]{2,1,0:T(8,128)}), f32[64,16,512]{2,1,0:T(8,128)S(1)}, u32[]{:S(2)}, u32[]{:S(2)}) async-start(f32[64,16,512]{2,1,0:T(8,128)} %copy-done.5), calls=%async_computation.3 | async-start | bytes 4194304 | tf_op jit(solution)/shard_map/all_to_all | solution.py:522
  175.3 25.3 %copy-start.3 = (f32[512,512]{1,0:T(8,128)S(1)}, f32[512,512]{1,0:T(8,128)}, u32[]{:S(2)}) copy-start(f32[512,512]{1,0:T(8,128)} %chol.1.li_ref) | copy-start | bytes 3145732
  175.3 25.3 %copy-start.10 = (s32[3]{0:T(128)S(1)}, s32[3]{0:T(128)}, u32[]{:S(2)}) copy-start(s32[3]{0:T(128)} %pad_add_fusion.pos) | copy-start | bytes 40
  175.3 25.3 %all-to-all-start.4 = ((f32[128,8,128]{2,1,0:T(8,128)}), f32[128,8,128]{2,1,0:T(8,128)S(1)}, u32[]{:S(2)}, u32[]{:S(2)}) async-start(f32[128,8,128]{2,1,0:T(8,128)} %half.1), calls=%async_computation.4 | async-start | bytes 1048576 | tf_op jit(solution)/shard_map/all_to_all | solution.py:522
  185.9 7.1 %collective-permute-start.7 = (f32[64,512]{1,0:T(8,128)}, f32[64,512]{1,0:T(8,128)S(1)}, u32[]{:S(2)}, u32[]{:S(2)}) collective-permute-start(f32[64,512]{1,0:T(8,128)} %get-tuple-element.81), channel_id=1, source_target_pairs={{0,1},{1,0},{2,3},{3,2},{4,5},{5,4},{6,7},{7,6},{8,9},{9,8},{10,11... | collective-permute-start | bytes 393224 | tf_op jit(solution)/shard_map/ppermute | solution.py:564
  187.3 11.8 %collective-permute-start.8 = (f32[64,512]{1,0:T(8,128)}, f32[64,512]{1,0:T(8,128)S(1)}, u32[]{:S(2)}, u32[]{:S(2)}) collective-permute-start(f32[64,512]{1,0:T(8,128)} %get-tuple-element.82), channel_id=1, source_target_pairs={{0,2},{1,3},{2,0},{3,1},{4,6},{5,7},{6,4},{7,5},{8,10},{9,11},{10,... | collective-permute-start | bytes 393224 | tf_op jit(solution)/shard_map/ppermute | solution.py:564
  189.7 23.1 %collective-permute-start.9 = (f32[64,512]{1,0:T(8,128)}, f32[64,512]{1,0:T(8,128)S(1)}, u32[]{:S(2)}, u32[]{:S(2)}) collective-permute-start(f32[64,512]{1,0:T(8,128)} %get-tuple-element.83), channel_id=1, source_target_pairs={{0,3},{1,2},{2,1},{3,0},{4,7},{5,6},{6,5},{7,4},{8,11},{9,10},{10,... | collective-permute-start | bytes 393224 | tf_op jit(solution)/shard_map/ppermute | solution.py:564
  189.7 23.0 %collective-permute-start.10 = (f32[64,512]{1,0:T(8,128)}, f32[64,512]{1,0:T(8,128)S(1)}, u32[]{:S(2)}, u32[]{:S(2)}) collective-permute-start(f32[64,512]{1,0:T(8,128)} %get-tuple-element.84), channel_id=1, source_target_pairs={{0,4},{1,5},{2,6},{3,7},{4,0},{5,1},{6,2},{7,3},{8,12},{9,13},{10,... | collective-permute-start | bytes 393224 | tf_op jit(solution)/shard_map/ppermute | solution.py:564
  193.0 19.7 %collective-permute-start.11 = (f32[64,512]{1,0:T(8,128)}, f32[64,512]{1,0:T(8,128)S(1)}, u32[]{:S(2)}, u32[]{:S(2)}) collective-permute-start(f32[64,512]{1,0:T(8,128)} %get-tuple-element.85), channel_id=1, source_target_pairs={{0,5},{1,4},{2,7},{3,6},{4,1},{5,0},{6,3},{7,2},{8,13},{9,12},{10,... | collective-permute-start | bytes 393224 | tf_op jit(solution)/shard_map/ppermute | solution.py:564
  193.0 19.7 %collective-permute-start.12 = (f32[64,512]{1,0:T(8,128)}, f32[64,512]{1,0:T(8,128)S(1)}, u32[]{:S(2)}, u32[]{:S(2)}) collective-permute-start(f32[64,512]{1,0:T(8,128)} %get-tuple-element.86), channel_id=1, source_target_pairs={{0,6},{1,7},{2,4},{3,5},{4,2},{5,3},{6,0},{7,1},{8,14},{9,15},{10,... | collective-permute-start | bytes 393224 | tf_op jit(solution)/shard_map/ppermute | solution.py:564
  199.1 13.7 %collective-permute-start.13 = (f32[64,512]{1,0:T(8,128)}, f32[64,512]{1,0:T(8,128)S(1)}, u32[]{:S(2)}, u32[]{:S(2)}) collective-permute-start(f32[64,512]{1,0:T(8,128)} %get-tuple-element.87), channel_id=1, source_target_pairs={{0,7},{1,6},{2,5},{3,4},{4,3},{5,2},{6,1},{7,0},{8,15},{9,14},{10,... | collective-permute-start | bytes 393224 | tf_op jit(solution)/shard_map/ppermute | solution.py:564
  203.2 19.4 %all-to-all-start.5 = ((f32[128,2,128]{2,1,0:T(2,128)}), f32[128,2,128]{2,1,0:T(2,128)S(1)}, u32[]{:S(2)}, u32[]{:S(2)}) async-start(f32[128,2,128]{2,1,0:T(2,128)} %get-tuple-element.91), calls=%async_computation.5 | async-start | bytes 262144 | tf_op jit(solution)/shard_map/all_to_all | solution.py:522
  (15 other events, 44.4 us)

commit v2 on v1

--- a/solution.py
+++ b/solution.py
@@ -558,9 +558,10 @@
     s = moments(pos,x,other,yt,ot,grid,plo,phi)
     s, g = lax.optimization_barrier((s,g))
     li = chol(g,1.0/NORB)
-    rows = swap(half(pos,swap(s,PEERS),li),ALL).reshape(8,2,64,128)
+    q = rotate(pos,x,li)
+    s, _ = lax.optimization_barrier((swap(s,PEERS),q[0]))
+    rows = swap(half(pos,s,li),ALL).reshape(8,2,64,128)
     projected, dipoles, spec = tile(pos,rows,li)
-    q = rotate(pos,x,li)
     q = [q[0]]+[lax.ppermute(q[r],"gy",[(i,i^r) for i in range(8)]) for r in range(1,8)]
     orthonormal = gather(pos,q).T
     spectrum = jnp.sum(swap(spec,ALL),axis=0).reshape(256)

time: 224 us -> 223 us (level)
    ppermute x7, waiting for transfers between devices: 0.02 us -> 2.71 us  [shards(): lax.ppermute(q[r], 'gy', [(i, i ^ r) for i in range(8)])]
    unnamed x40 -> x42, local copies, waits for them, and re-layouts: 16.2 us -> 14.8 us
  transfers between devices with their start and end apart: 19 -> 19, of which waited for: 7 -> 8; matrix products, arithmetic and copies ran while one was open for 0% -> 0% of each run, Pallas kernels for 22% -> 22%
where the time goes in v2:
time: 223 us; the launch traced here: 222 us
  Pallas kernels  74.4 us (33%)
  starting transfers between devices  73.1 us (33%)
  waiting for transfers between devices  31.3 us (14%)
  blocking collectives  24.8 us (11%)
  local copies, waits for them, and re-layouts  15.7 us (7%)
    all_to_all x5, starting transfers between devices, swap(): return lax.all_to_all(x, axis, split_axis=0, concat_axis=0, tiled=True)  38.7 us
    pallas_call x7, Pallas kernels, call(): pl.pallas_call(kernel, name=name, **grid, in_specs=[pl.BlockSpec(memory_s...  34.6 us
    all_to_all x1, blocking collectives, swap(): return lax.all_to_all(x, axis, split_axis=0, concat_axis=0, tiled=True)  24.8 us
    all_to_all x5, waiting for transfers between devices, swap(): return lax.all_to_all(x, axis, split_axis=0, concat_axis=0, tiled=True)  23 us
    pallas_call x3, Pallas kernels, step(): pl.pallas_call(functools.partial(step_kernel, first, wide, last), name='s...  18.3 us
    ppermute x7, starting transfers between devices, shards(): lax.ppermute(q[r], 'gy', [(i, i ^ r) for i in range(8)])  15.2 us
    unnamed x42, local copies, waits for them, and re-layouts  14.8 us
    ppermute x1, starting transfers between devices, shards(): ot = lax.ppermute(yt, SLABS, [(i + 1, i) for i in range(0, 16, 2)])  4.61 us
  transfers between devices with their start and end apart: 19, of which 8 were waited for; matrix products, arithmetic and copies ran while one was open for 0% of the time, Pallas kernels for 22%

profile of v2, /device:TPU:1, one launch (start us, length us, event | category | flops | bytes accessed | tf_op | source)
XLA Modules:
  0.0 221.6 jit_solution(16447825956063376576)
XLA Ops:
  1.3 3.5 %payload.1 = (f32[1568,128]{1,0:T(8,128)}, f32[1568,128]{1,0:T(8,128)}, f32[3,512]{1,0:T(4,128)}) custom-call(s32[3]{0:T(128)} %pad_add_fusion.pos, s32[5,32]{1,0:T(8,128)} %bitcast.20, f32[32,5,128,128]{3,2,1,0:T(8,128)} %hb.1, f32[32,5,128,128]{3,2,1,0:T(8,128)} %hb.1, f32[64,4096]{1,0:T(8,128)} %bitcast.10, f32[64,4096]{1,0:T(8,128)} %bitcast.11, ...), custom_call_target="tpu_custom_call" | custom-call | flops 1000000 | bytes 4194304 | tf_op jit(solution)/shard_map/payload/pallas_call | solution.py:151
  4.8 4.6 %collective-permute-start = (f32[1568,128]{1,0:T(8,128)}, f32[1568,128]{1,0:T(8,128)S(1)}, u32[]{:S(2)}, u32[]{:S(2)}) collective-permute-start(f32[1568,128]{1,0:T(8,128)} %get-tuple-element.50), channel_id=1, source_target_pairs={{0,8},{8,16},{16,24},{24,32},{32,40},{40,48},{48,56},{56,64},{64,7... | collective-permute-start | bytes 2408456 | tf_op jit(solution)/shard_map/ppermute | solution.py:534
  11.3 4.0 %copy-done = f32[32,5,128,128]{3,2,1,0:T(8,128)S(1)} copy-done((f32[32,5,128,128]{3,2,1,0:T(8,128)S(1)}, f32[32,5,128,128]{3,2,1,0:T(8,128)}, u32[]{:S(2)}) %copy-start) | copy-done | bytes 10485784
  15.3 3.6 %prep.1 = (bf16[32,256,640]{2,1,0:T(8,128)(2,1)S(1)}, f32[4096,128]{1,0:T(8,128)S(1)}, bf16[4096,128]{1,0:T(8,128)(2,1)S(1)}, bf16[4,256,640]{2,1,0:T(8,128)(2,1)S(1)}) custom-call(s32[3]{0:T(128)S(1)} %copy-done.9, f32[32,5,128,128]{3,2,1,0:T(8,128)S(1)} %copy-done, f32[64,4096]{1,0:T(8,128)S(1)} %bitcast.12), custom_call_target="tpu_custom_call" | custom-call | flops 1000000 | bytes 26214400 | tf_op jit(solution)/shard_map/prep/pallas_call | solution.py:124
  18.9 4.1 %collective-permute-done.1.hi_ref = f32[1568,128]{1,0:T(8,128)S(1)} collective-permute-done((f32[1568,128]{1,0:T(8,128)}, f32[1568,128]{1,0:T(8,128)S(1)}, u32[]{:S(2)}, u32[]{:S(2)}) %collective-permute-start.1) | collective-permute-done | bytes 802848 | tf_op jit(solution)/shard_map/ppermute | solution.py:535
  23.4 6.2 %step.3 = (f32[4096,128]{1,0:T(8,128)S(1)}, bf16[4096,128]{1,0:T(8,128)(2,1)S(1)}, f32[512,128]{1,0:T(8,128)S(1)}, bf16[512,128]{1,0:T(8,128)(2,1)S(1)}) custom-call(s32[3]{0:T(128)S(1)} %copy-done.9, s32[5,32]{1,0:T(8,128)S(1)} %bitcast.21, bf16[32,256,640]{2,1,0:T(8,128)(2,1)S(1)} %get-tuple-element.49.a2.alo.ahi, ...), custom_call_target="tpu_custom_call" | custom-call | flops 6039797760 | bytes 16777216 | tf_op jit(solution)/shard_map/step/pallas_call | solution.py:267
  35.5 4.4 %inner.1 = (f32[4096,128]{1,0:T(8,128)S(1)}, bf16[4096,128]{1,0:T(8,128)(2,1)S(1)}) custom-call(s32[3]{0:T(128)S(1)} %copy-done.9, s32[5,32]{1,0:T(8,128)S(1)} %bitcast.23, bf16[32,256,640]{2,1,0:T(8,128)(2,1)S(1)} %get-tuple-element.49.a2.alo.ahi, bf16[4096,128]{1,0:T(8,128)(2,1)S(1)} %get-tuple-element.57.vlo.vhi.p, f32[1024,128]{1,0:T(8,128)S(1)} %get-tuple-element.60.ye, ...), custom_call_target="tpu_custom_call" | custom-call | flops 4026531840 | bytes 16777216 | tf_op jit(solution)/shard_map/inner/pallas_call | solution.py:328
  40.1 6.2 %step.4 = (f32[4096,128]{1,0:T(8,128)S(1)}, bf16[4096,128]{1,0:T(8,128)(2,1)S(1)}, f32[512,128]{1,0:T(8,128)S(1)}, bf16[512,128]{1,0:T(8,128)(2,1)S(1)}) custom-call(s32[3]{0:T(128)S(1)} %copy-done.9, s32[5,32]{1,0:T(8,128)S(1)} %bitcast.24, bf16[32,256,640]{2,1,0:T(8,128)(2,1)S(1)} %get-tuple-element.49.a2.alo.ahi, ...), custom_call_target="tpu_custom_call" | custom-call | flops 6039797760 | bytes 16777216 | tf_op jit(solution)/shard_map/step/pallas_call | solution.py:267
  46.4 5.9 %step.5 = f32[8,64,512]{2,1,0:T(8,128)S(1)} custom-call(s32[3]{0:T(128)S(1)} %copy-done.9, s32[5,32]{1,0:T(8,128)S(1)} %bitcast.25, bf16[32,256,640]{2,1,0:T(8,128)(2,1)S(1)} %get-tuple-element.49.a2.alo.ahi, bf16[4,256,640]{2,1,0:T(8,128)(2,1)S(1)} %get-tuple-element.52.a2h, bf16[4096,128]{1,0:T(8,128)(2,1)S(1)} %get-tuple-element.68.p, ...), custom_call_target="tpu_custom_call" | custom-call | flops 6039797760 | bytes 16777216 | tf_op jit(solution)/shard_map/step/pallas_call | solution.py:267
  52.3 24.8 %all_to_all.30 = f32[8,64,512]{2,1,0:T(8,128)S(1)} all-to-all(f32[8,64,512]{2,1,0:T(8,128)S(1)} %step.5), channel_id=1, replica_groups=mesh['gq'=8,'c'=2,'gy'=8] {'gy'}, dimensions={0} | all-to-all | bytes 2097152 | tf_op jit(solution)/shard_map/all_to_all | solution.py:522
  85.0 8.9 %all-to-all-start.1 = ((f32[64,8,256]{2,1,0:T(8,128)}), f32[64,8,256]{2,1,0:T(8,128)S(1)}, u32[]{:S(2)}, u32[]{:S(2)}) async-start(f32[64,8,256]{2,1,0:T(8,128)} %copy-done.6), calls=%async_computation.1 | async-start | bytes 1048576 | tf_op jit(solution)/shard_map/all_to_all | solution.py:522
  95.4 3.8 %applied.1.yt_ref = f32[512,512]{1,0:T(8,128)S(1)} custom-call(s32[3]{0:T(128)S(1)} %copy-done.9, s32[5,32]{1,0:T(8,128)S(1)} %bitcast.26, f32[512,512]{1,0:T(8,128)S(1)} %bitcast.16, f32[512,256]{1,0:T(8,128)} %collective-permute-done.5.hi_ref, bf16[4,256,640]{2,1,0:T(8,128)(2,1)S(1)} %copy-done.12), custom_call_target="tpu_custom_call" | custom-call | flops 1342177280 | bytes 5242880 | tf_op jit(solution)/shard_map/applied/pallas_call | solution.py:381
  100.2 5.0 %all-to-all-done.1.p_ref = f32[64,8,256]{2,1,0:T(8,128)S(1)} async-done(((f32[64,8,256]{2,1,0:T(8,128)}), f32[64,8,256]{2,1,0:T(8,128)S(1)}, u32[]{:S(2)}, u32[]{:S(2)}) %all-to-all-start.1) | async-done | bytes 524320 | tf_op jit(solution)/shard_map/all_to_all | solution.py:522
  105.2 4.6 %collective-permute-start.6 = (f32[512,512]{1,0:T(8,128)}, f32[512,512]{1,0:T(8,128)S(1)}, u32[]{:S(2)}, u32[]{:S(2)}) collective-permute-start(f32[512,512]{1,0:T(8,128)} %copy-done.15), channel_id=1, source_target_pairs={{8,0},{24,16},{40,32},{56,48},{72,64},{88,80},{104,96},{120,112},{... | collective-permute-start | bytes 3145736 | tf_op jit(solution)/shard_map/ppermute | solution.py:555
  113.2 7.4 %all-to-all-start.2 = ((f32[128,8,256]{2,1,0:T(8,128)}), f32[128,8,256]{2,1,0:T(8,128)}, u32[]{:S(2)}, u32[]{:S(2)}) async-start(f32[128,8,256]{2,1,0:T(8,128)} %total.1), calls=%async_computation.2 | async-start | bytes 2097152 | tf_op jit(solution)/shard_map/all_to_all | solution.py:522
  124.3 4.0 %moments.1 = f32[64,16,512]{2,1,0:T(8,128)S(1)} custom-call(s32[3]{0:T(128)S(1)} %copy-done.9, f32[512,512]{1,0:T(8,128)S(1)} %bitcast.17, f32[512,512]{1,0:T(8,128)S(1)} %copy-done.14, f32[512,512]{1,0:T(8,128)S(1)} %copy-done.16, f32[512,512]{1,0:T(8,128)S(1)} %copy-done.18, f32[3,512]{1,0:T(4,128)S(1)} %copy-done.19, ...), custom_call_target="tpu_custom_call" | custom-call | flops 3221225472 | bytes 8388608 | tf_op jit(solution)/shard_map/moments/pallas_call | solution.py:421
  129.7 8.6 %all-to-all-done.2 = f32[128,8,256]{2,1,0:T(8,128)} async-done(((f32[128,8,256]{2,1,0:T(8,128)}), f32[128,8,256]{2,1,0:T(8,128)}, u32[]{:S(2)}, u32[]{:S(2)}) %all-to-all-start.2) | async-done | bytes 1048608 | tf_op jit(solution)/shard_map/all_to_all | solution.py:522
  138.2 5.9 %all-to-all-start.3 = ((f32[64,16,512]{2,1,0:T(8,128)}), f32[64,16,512]{2,1,0:T(8,128)S(1)}, u32[]{:S(2)}, u32[]{:S(2)}) async-start(f32[64,16,512]{2,1,0:T(8,128)} %copy-done.4), calls=%async_computation.3 | async-start | bytes 4194304 | tf_op jit(solution)/shard_map/all_to_all | solution.py:522
  144.1 22.8 %chol.1.li_ref = f32[512,512]{1,0:T(8,128)} custom-call(f32[8,2,64,256]{3,2,1,0:T(8,128)} %bitcast.6.g_ref), custom_call_target="tpu_custom_call" | custom-call | flops 8000000000 | bytes 4194304 | tf_op jit(solution)/shard_map/chol/pallas_call | solution.py:88
  166.9 3.3 %rotate.1 = (f32[64,512]{1,0:T(8,128)}, f32[64,512]{1,0:T(8,128)}, f32[64,512]{1,0:T(8,128)}, f32[64,512]{1,0:T(8,128)}, f32[64,512]{1,0:T(8,128)}, /*index=5*/f...) custom-call(s32[3]{0:T(128)} %pad_add_fusion.pos, f32[512,512]{1,0:T(8,128)} %bitcast.18, f32[512,512]{1,0:T(8,128)} %chol.1.li_ref), custom_call_target="tpu_custom_call" | custom-call | flops 805306368 | bytes 4194304 | tf_op jit(solution)/shard_map/rotate/pallas_call | solution.py:88
  174.0 8.6 %all-to-all-start.4 = ((f32[128,8,128]{2,1,0:T(8,128)}), f32[128,8,128]{2,1,0:T(8,128)S(1)}, u32[]{:S(2)}, u32[]{:S(2)}) async-start(f32[128,8,128]{2,1,0:T(8,128)} %copy-done.5), calls=%async_computation.4 | async-start | bytes 1048576 | tf_op jit(solution)/shard_map/all_to_all | solution.py:522
  192.6 5.2 %collective-permute-start.12 = (f32[64,512]{1,0:T(8,128)}, f32[64,512]{1,0:T(8,128)S(1)}, u32[]{:S(2)}, u32[]{:S(2)}) collective-permute-start(f32[64,512]{1,0:T(8,128)} %get-tuple-element.87), channel_id=1, source_target_pairs={{0,6},{1,7},{2,4},{3,5},{4,2},{5,3},{6,0},{7,1},{8,14},{9,15},{10,... | collective-permute-start | bytes 393224 | tf_op jit(solution)/shard_map/ppermute | solution.py:565
  203.2 7.9 %all-to-all-start.5 = ((f32[128,2,128]{2,1,0:T(2,128)}), f32[128,2,128]{2,1,0:T(2,128)S(1)}, u32[]{:S(2)}, u32[]{:S(2)}) async-start(f32[128,2,128]{2,1,0:T(2,128)} %get-tuple-element.93), calls=%async_computation.5 | async-start | bytes 262144 | tf_op jit(solution)/shard_map/all_to_all | solution.py:522
  212.7 8.2 %all-to-all-done.5 = f32[128,2,128]{2,1,0:T(2,128)S(1)} async-done(((f32[128,2,128]{2,1,0:T(2,128)}), f32[128,2,128]{2,1,0:T(2,128)S(1)}, u32[]{:S(2)}, u32[]{:S(2)}) %all-to-all-start.5) | async-done | bytes 131104 | tf_op jit(solution)/shard_map/all_to_all | solution.py:522
  (78 shorter events, 49.1 us)
Async XLA Ops:
  4.8 14.2 %collective-permute-start = (f32[1568,128]{1,0:T(8,128)}, f32[1568,128]{1,0:T(8,128)S(1)}, u32[]{:S(2)}, u32[]{:S(2)}) collective-permute-start(f32[1568,128]{1,0:T(8,128)} %get-tuple-element.50), channel_id=1, source_target_pairs={{0,8},{8,16},{16,24},{24,32},{32,40},{40,48},{48,56},{56,64},{64,7... | collective-permute-start | bytes 2408456 | tf_op jit(solution)/shard_map/ppermute | solution.py:534
  9.3 13.7 %collective-permute-start.1 = (f32[1568,128]{1,0:T(8,128)}, f32[1568,128]{1,0:T(8,128)S(1)}, u32[]{:S(2)}, u32[]{:S(2)}) collective-permute-start(f32[1568,128]{1,0:T(8,128)} %get-tuple-element.51), channel_id=1, source_target_pairs={{8,0},{16,8},{24,16},{32,24},{40,32},{48,40},{56,48},{64,56},{72,6... | collective-permute-start | bytes 2408456 | tf_op jit(solution)/shard_map/ppermute | solution.py:535
  18.9 10.7 %copy-start.11 = (bf16[4,256,640]{2,1,0:T(8,128)(2,1)}, bf16[4,256,640]{2,1,0:T(8,128)(2,1)S(1)}, u32[]{:S(2)}) copy-start(bf16[4,256,640]{2,1,0:T(8,128)(2,1)S(1)} %get-tuple-element.74.a2) | copy-start | bytes 3932164
  31.2 8.8 %collective-permute-start.2 = (f32[256,128]{1,0:T(8,128)S(1)}, f32[256,128]{1,0:T(8,128)S(1)}, u32[]{:S(2)}, u32[]{:S(2)}) collective-permute-start(f32[256,128]{1,0:T(8,128)S(1)} %get-tuple-element.62), channel_id=1, source_target_pairs={{0,8},{8,16},{16,24},{24,32},{32,40},{40,48},{48,56},{56,64},{64,7... | collective-permute-start | bytes 393224 | tf_op jit(solution)/shard_map/ppermute | solution.py:540
  33.1 6.9 %collective-permute-start.3 = (f32[256,128]{1,0:T(8,128)S(1)}, f32[256,128]{1,0:T(8,128)S(1)}, u32[]{:S(2)}, u32[]{:S(2)}) collective-permute-start(f32[256,128]{1,0:T(8,128)S(1)} %get-tuple-element.63), channel_id=1, source_target_pairs={{8,0},{16,8},{24,16},{32,24},{40,32},{48,40},{56,48},{64,56},{72,6... | collective-permute-start | bytes 393224 | tf_op jit(solution)/shard_map/ppermute | solution.py:541
  77.1 43.5 %copy-start.3 = (f32[8,64,512]{2,1,0:T(8,128)}, f32[8,64,512]{2,1,0:T(8,128)S(1)}, u32[]{:S(2)}) copy-start(f32[8,64,512]{2,1,0:T(8,128)S(1)} %all_to_all.30) | copy-start | bytes 3145732
  77.1 4.5 %collective-permute-start.4 = (f32[512,512]{1,0:T(8,128)S(1)}, f32[512,512]{1,0:T(8,128)S(1)}, u32[]{:S(2)}, u32[]{:S(2)}) collective-permute-start(f32[512,512]{1,0:T(8,128)S(1)} %bitcast.13), channel_id=1, source_target_pairs={{0,8},{8,0},{16,24},{24,16},{32,40},{40,32},{48,56},{56,48},{64,72... | collective-permute-start | bytes 3145736 | tf_op jit(solution)/shard_map/ppermute | solution.py:549
  78.4 15.7 %collective-permute-start.5 = (f32[512,256]{1,0:T(8,128)}, f32[512,256]{1,0:T(8,128)}, u32[]{:S(2)}, u32[]{:S(2)}) collective-permute-start(f32[512,256]{1,0:T(8,128)} %slice.4), channel_id=1, source_target_pairs={{1,0},{2,1},{3,2},{4,3},{5,4},{6,5},{7,6},{8,7},{9,8},{10,9},{11,1... | collective-permute-start | bytes 1572872 | tf_op jit(solution)/shard_map/ppermute | solution.py:550
  85.0 20.2 %all-to-all-start.1 = ((f32[64,8,256]{2,1,0:T(8,128)}), f32[64,8,256]{2,1,0:T(8,128)S(1)}, u32[]{:S(2)}, u32[]{:S(2)}) async-start(f32[64,8,256]{2,1,0:T(8,128)} %copy-done.6), calls=%async_computation.1 | async-start | bytes 1048576 | tf_op jit(solution)/shard_map/all_to_all | solution.py:522
  100.2 20.4 %copy-start.19 = (f32[3,512]{1,0:T(4,128)S(1)}, f32[3,512]{1,0:T(4,128)}, u32[]{:S(2)}) copy-start(f32[3,512]{1,0:T(4,128)} %get-tuple-element.78.g_ref) | copy-start | bytes 18436
  105.2 7.0 %collective-permute-start.6 = (f32[512,512]{1,0:T(8,128)}, f32[512,512]{1,0:T(8,128)S(1)}, u32[]{:S(2)}, u32[]{:S(2)}) collective-permute-start(f32[512,512]{1,0:T(8,128)} %copy-done.15), channel_id=1, source_target_pairs={{8,0},{24,16},{40,32},{56,48},{72,64},{88,80},{104,96},{120,112},{... | collective-permute-start | bytes 3145736 | tf_op jit(solution)/shard_map/ppermute | solution.py:555
  113.2 25.1 %all-to-all-start.2 = ((f32[128,8,256]{2,1,0:T(8,128)}), f32[128,8,256]{2,1,0:T(8,128)}, u32[]{:S(2)}, u32[]{:S(2)}) async-start(f32[128,8,256]{2,1,0:T(8,128)} %total.1), calls=%async_computation.2 | async-start | bytes 2097152 | tf_op jit(solution)/shard_map/all_to_all | solution.py:522
  138.2 33.3 %all-to-all-start.3 = ((f32[64,16,512]{2,1,0:T(8,128)}), f32[64,16,512]{2,1,0:T(8,128)S(1)}, u32[]{:S(2)}, u32[]{:S(2)}) async-start(f32[64,16,512]{2,1,0:T(8,128)} %copy-done.4), calls=%async_computation.3 | async-start | bytes 4194304 | tf_op jit(solution)/shard_map/all_to_all | solution.py:522
  171.5 26.3 %copy-start.20 = (f32[64,512]{1,0:T(8,128)S(1)}, f32[64,512]{1,0:T(8,128)}, u32[]{:S(2)}) copy-start(f32[64,512]{1,0:T(8,128)} %get-tuple-element.88) | copy-start | bytes 393220
  174.0 37.1 %copy-start.7 = (f32[64,512]{1,0:T(8,128)S(1)}, f32[64,512]{1,0:T(8,128)}, u32[]{:S(2)}) copy-start(f32[64,512]{1,0:T(8,128)} %get-tuple-element.81.refs_0_) | copy-start | bytes 393220
  174.0 26.6 %all-to-all-start.4 = ((f32[128,8,128]{2,1,0:T(8,128)}), f32[128,8,128]{2,1,0:T(8,128)S(1)}, u32[]{:S(2)}, u32[]{:S(2)}) async-start(f32[128,8,128]{2,1,0:T(8,128)} %copy-done.5), calls=%async_computation.4 | async-start | bytes 1048576 | tf_op jit(solution)/shard_map/all_to_all | solution.py:522
  182.7 9.9 %collective-permute-start.7 = (f32[64,512]{1,0:T(8,128)}, f32[64,512]{1,0:T(8,128)S(1)}, u32[]{:S(2)}, u32[]{:S(2)}) collective-permute-start(f32[64,512]{1,0:T(8,128)} %get-tuple-element.82), channel_id=1, source_target_pairs={{0,1},{1,0},{2,3},{3,2},{4,5},{5,4},{6,7},{7,6},{8,9},{9,8},{10,11... | collective-permute-start | bytes 393224 | tf_op jit(solution)/shard_map/ppermute | solution.py:565
  184.1 13.7 %collective-permute-start.8 = (f32[64,512]{1,0:T(8,128)}, f32[64,512]{1,0:T(8,128)S(1)}, u32[]{:S(2)}, u32[]{:S(2)}) collective-permute-start(f32[64,512]{1,0:T(8,128)} %get-tuple-element.83), channel_id=1, source_target_pairs={{0,2},{1,3},{2,0},{3,1},{4,6},{5,7},{6,4},{7,5},{8,10},{9,11},{10,... | collective-permute-start | bytes 393224 | tf_op jit(solution)/shard_map/ppermute | solution.py:565
  186.5 24.5 %collective-permute-start.9 = (f32[64,512]{1,0:T(8,128)}, f32[64,512]{1,0:T(8,128)S(1)}, u32[]{:S(2)}, u32[]{:S(2)}) collective-permute-start(f32[64,512]{1,0:T(8,128)} %get-tuple-element.84), channel_id=1, source_target_pairs={{0,3},{1,2},{2,1},{3,0},{4,7},{5,6},{6,5},{7,4},{8,11},{9,10},{10,... | collective-permute-start | bytes 393224 | tf_op jit(solution)/shard_map/ppermute | solution.py:565
  186.6 24.5 %collective-permute-start.10 = (f32[64,512]{1,0:T(8,128)}, f32[64,512]{1,0:T(8,128)S(1)}, u32[]{:S(2)}, u32[]{:S(2)}) collective-permute-start(f32[64,512]{1,0:T(8,128)} %get-tuple-element.85), channel_id=1, source_target_pairs={{0,4},{1,5},{2,6},{3,7},{4,0},{5,1},{6,2},{7,3},{8,12},{9,13},{10,... | collective-permute-start | bytes 393224 | tf_op jit(solution)/shard_map/ppermute | solution.py:565
  189.9 21.2 %collective-permute-start.11 = (f32[64,512]{1,0:T(8,128)}, f32[64,512]{1,0:T(8,128)S(1)}, u32[]{:S(2)}, u32[]{:S(2)}) collective-permute-start(f32[64,512]{1,0:T(8,128)} %get-tuple-element.86), channel_id=1, source_target_pairs={{0,5},{1,4},{2,7},{3,6},{4,1},{5,0},{6,3},{7,2},{8,13},{9,12},{10,... | collective-permute-start | bytes 393224 | tf_op jit(solution)/shard_map/ppermute | solution.py:565
  192.6 18.5 %collective-permute-start.12 = (f32[64,512]{1,0:T(8,128)}, f32[64,512]{1,0:T(8,128)S(1)}, u32[]{:S(2)}, u32[]{:S(2)}) collective-permute-start(f32[64,512]{1,0:T(8,128)} %get-tuple-element.87), channel_id=1, source_target_pairs={{0,6},{1,7},{2,4},{3,5},{4,2},{5,3},{6,0},{7,1},{8,14},{9,15},{10,... | collective-permute-start | bytes 393224 | tf_op jit(solution)/shard_map/ppermute | solution.py:565
  197.8 13.3 %collective-permute-start.13 = (f32[64,512]{1,0:T(8,128)S(1)}, f32[64,512]{1,0:T(8,128)S(1)}, u32[]{:S(2)}, u32[]{:S(2)}) collective-permute-start(f32[64,512]{1,0:T(8,128)S(1)} %copy-done.20), channel_id=1, source_target_pairs={{0,7},{1,6},{2,5},{3,4},{4,3},{5,2},{6,1},{7,0},{8,15},{9,14},{10,... | collective-permute-start | bytes 393224 | tf_op jit(solution)/shard_map/ppermute | solution.py:565
  203.2 17.7 %all-to-all-start.5 = ((f32[128,2,128]{2,1,0:T(2,128)}), f32[128,2,128]{2,1,0:T(2,128)S(1)}, u32[]{:S(2)}, u32[]{:S(2)}) async-start(f32[128,2,128]{2,1,0:T(2,128)} %get-tuple-element.93), calls=%async_computation.5 | async-start | bytes 262144 | tf_op jit(solution)/shard_map/all_to_all | solution.py:522
  (16 other events, 52.2 us)
